TPU v7x, 256 devices: a whole 4x4x8 slice. The times are simulated.
256 devices in a mesh: ctx: 64 (over z, x, core), tp: 4 (over y).
Axes of the slice: x: 4, y: 4, z: 8, core: 2. Of those that a mesh axis runs over, the one named last changes fastest.
Arguments:
- query_one: bfloat16 [12288, 4096], P('ctx', 'tp'), may hold values from -64 to 64
- key_one: bfloat16 [12288, 1024], P('ctx', 'tp'), may hold values from -6 to 6
- value_one: bfloat16 [12288, 1024], P('ctx', 'tp'), may hold values from -6 to 6
- segments: int32 [12288], P('ctx'), may hold values from 0 to 3, never falling along the last dimension, each value on 1 to 6144 neighbouring positions
- query_base: bfloat16 [12288, 4096], P('ctx', 'tp'), may hold values from -20 to 20
- key_two: bfloat16 [12288, 1024], P('ctx', 'tp'), may hold values from -3 to 3
- value_two: bfloat16 [12288, 1024], P('ctx', 'tp'), may hold values from -64 to 64
Outputs:
- attended: bfloat16 [12288, 4096], P('ctx', 'tp')
Inputs may be any that keep to these rules, and one draw needn't show every extreme that they name: `segments`: document numbers never fall along the sequence; each of the 4 documents has 1 to 6144 tokens, one exactly that many.
All inputs are finite; a program needn't handle non-finite values.
Results may differ from a plain program's by a relative error of at most 0.0075.
Values may be sent and summed in bfloat16 or wider, within the bound.
No kernel may reach another device: no remote copies, remote signals or barrier semaphores. Data moves between devices by JAX's collectives and lax.ppermute only.
A program may use at most 192 MiB of HBM per device.

v0:
```python
from functools import partial

import jax
import jax.numpy as jnp
from jax import lax
from jax.sharding import PartitionSpec as P

HEAD_DIM = 128
WIDTH = 4096


EPSILON = 1e-05
NEGATIVE = -1e30
HIGHEST = lax.Precision.HIGHEST


def keep_carry(carried):
    return carried


def state_of_last(key_one, value_one, doc_ids, groups):
    tok_rows = doc_ids.shape[0]
    in_last = (doc_ids == doc_ids[tok_rows - 1])[:, None]
    masked = jnp.where(in_last, key_one, jnp.zeros_like(key_one)).reshape(
        tok_rows, groups, HEAD_DIM
    )
    return jnp.einsum(
        "rgd,rge->gde",
        masked,
        value_one.reshape(tok_rows, groups, HEAD_DIM),
        preferred_element_type=jnp.float32,
    )


def linear_local(query_one, key_one, value_one, doc_ids, prefix_state, groups):
    tok_rows = doc_ids.shape[0]
    repeat = query_one.shape[1] // (groups * HEAD_DIM)
    queries = query_one.reshape(tok_rows, groups, repeat, HEAD_DIM)
    scores = jnp.einsum(
        "rgpd,sgd->gprs",
        queries,
        key_one.reshape(tok_rows, groups, HEAD_DIM),
        preferred_element_type=jnp.float32,
    )
    places = jnp.arange(tok_rows, dtype=jnp.int32)
    visible = (places[None, :] <= places[:, None]) & (doc_ids[None, :] == doc_ids[:, None])
    scores = jnp.where(visible, scores, 0.0)
    values_wide = value_one.reshape(tok_rows, groups, HEAD_DIM).astype(jnp.float32)
    inside = jnp.einsum("gprs,sge->rgpe", scores, values_wide, precision=HIGHEST)
    earlier = jnp.einsum(
        "rgpd,gde->rgpe", queries.astype(jnp.float32), prefix_state, precision=HIGHEST
    )
    earlier = jnp.where((doc_ids == doc_ids[0])[:, None, None, None], earlier, 0.0)
    return (inside + earlier).reshape(tok_rows, -1)


def softmax_update(carried, queries, query_pos, query_doc, keys_now, values_now, key_pos, key_doc):
    top_scores, totals, summed = carried
    scores = jnp.einsum(
        "rgpd,sgd->gprs", queries, keys_now, preferred_element_type=jnp.float32
    ) * HEAD_DIM ** (-0.5)
    visible = (key_pos[None, :] <= query_pos[:, None]) & (key_doc[None, :] == query_doc[:, None])
    scores = jnp.where(visible, scores, NEGATIVE)
    new_top = jnp.maximum(top_scores, jnp.max(scores, axis=-1))
    weights = jnp.where(visible, jnp.exp(scores - new_top[..., None]), 0.0)
    totals = jnp.sum(weights, axis=-1)
    summed = jnp.einsum(
        "gprs,sge->gpre",
        weights.astype(jnp.bfloat16),
        values_now,
        preferred_element_type=jnp.float32,
    )
    return (new_top, totals, summed)


def attention_parts(query_rows, query_pos, query_doc, key_two, key_docs, splits):
    tok_rows = query_pos.shape[0]
    groups = key_two.shape[1] // HEAD_DIM
    repeat = query_rows.shape[1] // (groups * HEAD_DIM)
    queries = query_rows.reshape(tok_rows, groups, repeat, HEAD_DIM)
    part_rows = tok_rows // splits
    total_keys = key_docs.shape[0]
    padded_docs = jnp.concatenate(
        [jnp.full((total_keys,), -1, jnp.int32), key_docs.astype(jnp.int32)], axis=0
    )
    sections = []
    sections.append((queries, query_pos, query_doc))
    start_carry = tuple(
        (
            (
                jnp.full((groups, repeat, part_rows), NEGATIVE, jnp.float32),
                jnp.zeros((groups, repeat, part_rows), jnp.float32),
                jnp.zeros((groups, repeat, part_rows, HEAD_DIM), jnp.float32),
            )
            for section_index in range(splits)
        )
    )

    def absorb(carries, piece, start):
        keys_now, values_now = piece
        key_rows = keys_now.shape[0]
        key_pos = jnp.arange(key_rows, dtype=jnp.int32)
        key_doc = lax.dynamic_slice_in_dim(padded_docs, total_keys, key_rows)
        keys_grouped = keys_now.reshape(key_rows, groups, HEAD_DIM)
        values_grouped = values_now.reshape(key_rows, groups, HEAD_DIM)
        updated = []
        for carried, section in zip(carries, sections):
            block_queries, block_pos, block_doc = section
            needed = (
                (start <= jnp.max(block_pos))
                & (key_doc[0] <= jnp.max(block_doc))
                & (key_doc[key_rows - 1] >= jnp.min(block_doc))
            )
            updater = partial(
                softmax_update,
                queries=block_queries,
                query_pos=block_pos,
                query_doc=block_doc,
                keys_now=keys_grouped,
                values_now=values_grouped,
                key_pos=key_pos,
                key_doc=key_doc,
            )
            updated.append(lax.cond(needed, updater, keep_carry, carried))
        return tuple(updated)

    def finish(finals):
        outputs = []
        for top_scores, totals, summed in finals:
            outputs.append(
                jnp.transpose(summed / totals[..., None], (2, 0, 1, 3)).reshape(part_rows, -1)
            )
        return outputs[0].astype(jnp.bfloat16)

    return (absorb, start_carry, finish)


def shards(query_one, key_one, value_one, segments, query_base, key_two, value_two):
    tok_rows = segments.shape[0]
    groups = key_one.shape[1] // HEAD_DIM
    devices = lax.axis_size("ctx")
    my_index = lax.axis_index("ctx")
    first_doc = segments[0]
    own_state = state_of_last(key_one, value_one, segments, groups)
    all_states, key_docs = (
        lax.all_gather(own_state[None].astype(jnp.bfloat16), "ctx", axis=0, tiled=True).astype(
            jnp.float32
        ),
        lax.all_gather(segments, "ctx", axis=0, tiled=True),
    )
    last_docs = key_docs.reshape(devices, tok_rows)[:, tok_rows - 1]
    chosen = (jnp.arange(devices, dtype=jnp.int32) < my_index) & (last_docs == first_doc)
    prefix_state = jnp.sum(jnp.where(chosen[:, None, None, None], all_states, 0.0), axis=0)
    first_out = linear_local(query_one, key_one, value_one, segments, prefix_state, groups)
    width_sum = lax.psum(jnp.sum(first_out * first_out, axis=1), "tp")
    query_two = (
        query_base.astype(jnp.float32) + first_out * lax.rsqrt(width_sum / WIDTH + EPSILON)[:, None]
    ).astype(jnp.bfloat16)
    query_pos = my_index * tok_rows + jnp.arange(tok_rows, dtype=jnp.int32)
    absorb, start_carry, finish = attention_parts(
        query_two, query_pos, segments, key_two, key_docs, 1
    )
    finals = absorb(
        start_carry,
        (
            lax.all_gather(key_two, "ctx", axis=0, tiled=True),
            lax.all_gather(value_two, "ctx", axis=0, tiled=True),
        ),
        jnp.int32(0),
    )
    second_out = finish(finals)
    widened = second_out.astype(jnp.float32)
    out_sum = lax.psum(jnp.sum(widened * widened, axis=1), "tp")
    return (widened * lax.rsqrt(out_sum / WIDTH + EPSILON)[:, None]).astype(jnp.bfloat16)


def solution(mesh):
    in_specs = (
        P("ctx", "tp"),
        P("ctx", "tp"),
        P("ctx", "tp"),
        P("ctx"),
        P("ctx", "tp"),
        P("ctx", "tp"),
        P("ctx", "tp"),
    )
    out_specs = P("ctx", "tp")
    return jax.shard_map(shards, mesh=mesh, in_specs=in_specs, out_specs=out_specs, check_vma=False)
```

profile of v0, /device:TPU:8, one launch (start us, length us, event | category | flops | bytes accessed | tf_op | source)
XLA Modules:
  0.0 428.9 jit_solution(13717419977795824852)
XLA Ops:
  6.5 1.4 fusion.37
  7.9 2.0 broadcast_compare_fusion
  9.9 1.9 convolution_convert_fusion
  13.3 0.9 reshape.62
  14.2 0.9 reshape.64
  15.2 1.3 dynamic-slice
  17.1 0.9 dynamic-update-slice
  18.0 254.7 %all-reduce = s32[12288]{0:T(1024)S(1)} all-reduce(s32[12288]{0:T(1024)S(1)} %dynamic-update-slice), channel_id=1, replica_groups=mesh['ctx'=64,'tp'=4] {'ctx'}, use_global_device_ids=true, to_apply=%add | all-reduce | flops 12288 | bytes 98304
  272.7 1.3 reshape.63
  275.3 1.4 fusion.35
  279.6 0.8 fusion.32
  280.4 0.9 fusion.24
  281.7 1.6 fusion.15
  283.4 3.3 fusion.13
  288.2 8.8 %psum.14 = f32[192]{0:T(256)S(1)} all-reduce(f32[192]{0:T(256)S(1)} %get-tuple-element.45), channel_id=1, replica_groups=mesh['ctx'=64,'tp'=4] {'tp'}, use_global_device_ids=true, to_apply=%region_5.6 | all-reduce | flops 192 | bytes 1536 | tf_op jit(solution)/shard_map/psum | solution.py:155
  297.2 112.9 %conditional.1 = (f32[2,4,192]{2,1,0:T(4,128)S(1)}, f32[2,4,192,128]{3,2,1,0:T(8,128)S(1)}) conditional(s32[]{:T(128)} %convert_element_type.46, () %tuple.13, (s32[12288]{0:T(1024)S(1)}, s32[192]{0:T(256)S(1)}, s32[12288]{0:T(1024)}, s32[192]{0:T(256)S(1)}, bf16[12288,256]{1,0:T(8,128)(2,1)}, /*index=5*/bf16[192,1024]{1,0:T(8,128)(2,1)S(1)}, ...), branch_computations={%region_6.7_spmd, %region_7.10_spmd} | conditional | flops 9916119040 | bytes 275781120 | solution.py:124
  297.3 2.7 compare_and_fusion
  300.0 9.9 %reshape.53 = bf16[12288,2,128]{2,1,0:T(2,128)(2,1)} reshape(bf16[12288,256]{1,0:T(8,128)(2,1)} %get-tuple-element.26) | data formatting | bytes 12582912 | tf_op jit(solution)/shard_map/reshape | solution.py:104
  310.1 29.6 %fusion = (f32[2,4,192]{2,1,0:T(4,128)S(1)}, f32[2,12288,192,4]{1,2,3,0:T(8,128)}) fusion(pred[192,12288]{1,0:T(8,128)(4,1)S(1)} %compare_and_fusion, bf16[192,2,4,128]{3,2,1,0:T(4,128)(2,1)S(1)} %reshape.54, bf16[12288,2,128,1]{2,1,0,3:T(2,128)(2,1)} %bitcast.56), kind=kOutput, calls=%fused_computation.2 | convolution fusion | flops 4888459776 | bytes 84547584 | tf_op jit(solution)/shard_map/cond/branch_1_fun/rgpd,sgd->gprs/dot_general | solution.py:59
  339.7 9.7 %reshape.55 = bf16[12288,2,128]{2,1,0:T(2,128)(2,1)} reshape(bf16[12288,256]{1,0:T(8,128)(2,1)} %get-tuple-element.28) | data formatting | bytes 12582912 | tf_op jit(solution)/shard_map/reshape | solution.py:105
  349.4 32.3 %fusion.3 = f32[2,4,192,128]{3,2,1,0:T(8,128)S(1)} fusion(f32[2,12288,192,4]{1,2,3,0:T(8,128)} %get-tuple-element.38, f32[2,4,192]{2,1,0:T(4,128)S(1)} %broadcast_maximum_fusion, pred[192,12288]{1,0:T(8,128)(4,1)S(1)} %compare_and_fusion, bf16[12288,2,128,1]{2,1,0,3:T(2,128)(2,1)} %bitcast.57), kind=kOutput, calls=%fused_computation.5 | convolution fusion | flops 4926210048 | bytes 84940800 | tf_op jit(solution)/shard_map/cond/branch_1_fun/gprs,sge->gpre/dot_general | solution.py:67
  381.7 28.2 %fusion.2 = f32[2,4,192]{2,1,0:T(4,128)S(1)} fusion(f32[2,12288,192,4]{1,2,3,0:T(8,128)} %get-tuple-element.38, f32[2,4,192]{2,1,0:T(4,128)S(1)} %broadcast_maximum_fusion, pred[192,12288]{1,0:T(8,128)(4,1)S(1)} %compare_and_fusion), kind=kLoop, calls=%fused_computation.4 | loop fusion | flops 94370304 | bytes 77869056 | tf_op jit(solution)/shard_map/cond/branch_1_fun/reduce_sum | solution.py:66
  411.4 10.1 %psum.15 = f32[192]{0:T(256)S(1)} all-reduce(f32[192]{0:T(256)S(1)} %get-tuple-element.35), channel_id=1, replica_groups=mesh['ctx'=64,'tp'=4] {'tp'}, use_global_device_ids=true, to_apply=%region_11.12 | all-reduce | flops 192 | bytes 1536 | tf_op jit(solution)/shard_map/psum | solution.py:173
  421.5 0.9 multiply_convert_fusion
  (35 shorter events, 6.5 us)
Async XLA Ops:
  6.5 290.7 %copy-start.2 = (s32[192]{0:T(256)S(1)}, s32[192]{0:T(256)}, u32[]{:S(2)}) copy-start(s32[192]{0:T(256)} %param.12) | copy-start | bytes 2308
  6.5 290.4 %copy-start.1 = (bf16[192,1024]{1,0:T(8,128)(2,1)S(1)}, bf16[192,1024]{1,0:T(8,128)(2,1)}, u32[]{:S(2)}) copy-start(bf16[192,1024]{1,0:T(8,128)(2,1)} %param.13) | copy-start | bytes 1179652
  6.5 276.8 %all-gather.9.cloned.1.call-start = ((), (), s32[]{:S(2)}) async-start(), calls=%async_computation.2 | async-start | bytes 4259840 | tf_op jit(solution)/shard_map/all_gather | solution.py:146
  11.8 285.4 %all-gather.5.cloned.1.call-start = ((), (), s32[]{:S(2)}) async-start(), calls=%async_computation | async-start | bytes 6389760 | tf_op jit(solution)/shard_map/all_gather | solution.py:166
  12.6 284.6 %all-gather.7.cloned.1.call-start = ((), (), s32[]{:S(2)}) async-start(), calls=%async_computation.1 | async-start | bytes 6389760 | tf_op jit(solution)/shard_map/all_gather | solution.py:167
  272.6 9.1 %copy-start = (s32[12288]{0:T(1024)}, s32[12288]{0:T(1024)S(1)}, u32[]{:S(2)}) copy-start(s32[12288]{0:T(1024)S(1)} %all-reduce) | copy-start | bytes 147460
Sparse Core Ops, SparseCore 0:
  11.9 81.9 all-gather.8
  96.7 78.3 all-gather.4
  177.8 77.7 all-gather.6
where the time goes:
time: 430 us; the launch traced here: 429 us
  blocking collectives  274 us (64%)
  matrix products  66.3 us (15%)
  other arithmetic  41.4 us (10%)
  local copies, waits for them, and re-layouts  28.9 us (7%)
  between operations  16.9 us (4%)
    unnamed x1, blocking collectives  255 us
    dot_general x1, matrix products, softmax_update(): jnp.einsum('gprs,sge->gpre', weights.astype(jnp.bfloat16), values_now, pr...  32.3 us
    dot_general x1, matrix products, softmax_update(): jnp.einsum('rgpd,sgd->gprs', queries, keys_now, preferred_element_type=jn...  29.6 us
    reduce_sum x1, other arithmetic, softmax_update(): totals = jnp.sum(weights, axis=-1)  28.2 us
    psum x1, blocking collectives, shards(): out_sum = lax.psum(jnp.sum(widened * widened, axis=1), 'tp')  10.1 us
    reshape x1, local copies, waits for them, and re-layouts, absorb(): keys_grouped = keys_now.reshape(key_rows, groups, HEAD_DIM)  9.92 us
    reshape x1, local copies, waits for them, and re-layouts, absorb(): values_grouped = values_now.reshape(key_rows, groups, HEAD_DIM)  9.74 us
    psum x1, blocking collectives, shards(): width_sum = lax.psum(jnp.sum(first_out * first_out, axis=1), 'tp')  8.81 us
  transfers between devices with their start and end apart: 3, of which 0 were waited for; matrix products, arithmetic and copies ran while one was open for 4% of the time, Pallas kernels for 0%

commit v1 on v0

v1 whole, which is shorter than its diff:
```python
import jax
import jax.numpy as jnp
from jax import lax
from jax.experimental import pallas as pl
from jax.experimental.pallas import tpu as pltpu
from jax.sharding import PartitionSpec as P

HEAD_DIM = 128
WIDTH = 4096
EPSILON = 1e-05
NEGATIVE = -1e30

TOK = 192
PAIR = 384
REPEAT = 4
COLS = REPEAT * HEAD_DIM
Z, X, CORES, TP = 8, 4, 2, 4
BACK = 4
PRIOR = 16 * PAIR
CHUNK = 768
SCALE = HEAD_DIM ** (-0.5) * 1.4426950408889634

F32 = jnp.float32
BF16 = jnp.bfloat16
VMEM = pl.BlockSpec(memory_space=pltpu.VMEM)
SMEM = pl.BlockSpec(memory_space=pltpu.SMEM)
ANY = pl.BlockSpec(memory_space=pl.ANY)


def place():
    index = lax.axis_index("ctx")
    return index // (X * CORES), (index // CORES) % X, index % CORES


def call(kernel, outs, specs_in, specs_out, scratch=(), limit=None, name=None):
    return pl.pallas_call(
        kernel,
        out_shape=outs,
        in_specs=specs_in,
        out_specs=specs_out,
        scratch_shapes=list(scratch),
        compiler_params=pltpu.CompilerParams(vmem_limit_bytes=limit or 16 * 2**20),
        name=name,
    )


def count_below(ref, doc):
    found = jnp.int32(0)
    for step in (128, 64, 32, 16, 8, 4, 2, 1):
        tried = found + step
        last = ref[jnp.minimum(tried, TOK) - 1]
        found = jnp.where((tried <= TOK) & (last < doc), tried, found)
    return found


def half(core):
    return pl.ds(pl.multiple_of(core * HEAD_DIM, HEAD_DIM), HEAD_DIM)


def rows_of(core):
    return pl.ds(pl.multiple_of(core * TOK, 64), TOK)


def prep_kernel(
    seg, seg_r, k1, k1_r, v1, v1_r, k2, k2_r, v2, v2_r, pack_ref, state_ref, info_ref
):
    core = place()[2]
    mine, theirs = rows_of(core), rows_of(1 - core)
    pack_ref[mine, :HEAD_DIM] = k2[:, half(core)]
    pack_ref[mine, HEAD_DIM:] = v2[:, half(core)]
    pack_ref[theirs, :HEAD_DIM] = k2_r[:, half(core)]
    pack_ref[theirs, HEAD_DIM:] = v2_r[:, half(core)]
    below = [count_below(seg, d) for d in (1, 2, 3)]
    below_r = [count_below(seg_r, d) for d in (1, 2, 3)]
    bounds = [a + b for a, b in zip(below, below_r)]
    first = jnp.where(core == 0, seg[0], seg_r[0])
    last = jnp.where(core == 0, seg_r[TOK - 1], seg[TOK - 1])

    def pick(values, doc):
        out = jnp.int32(0)
        for d in (1, 2, 3):
            out = jnp.where(doc == d, values[d - 1], out)
        return out

    count = PAIR - pick(bounds, last)
    first_end = jnp.where(first == 3, PAIR, pick(bounds, first + 1))
    for place_in, value in enumerate((*bounds, first, last, count, first_end, 0)):
        info_ref[place_in] = jnp.int32(value)
    rows = lax.broadcasted_iota(jnp.int32, (TOK, HEAD_DIM), 0)
    state = jnp.zeros((HEAD_DIM, HEAD_DIM), F32)
    for keys, values, start in ((k1, v1, pick(below, last)), (k1_r, v1_r, pick(below_r, last))):
        masked = jnp.where(rows >= start, keys[:, half(core)].astype(F32), 0.0).astype(BF16)
        state += lax.dot_general(
            masked, values[:, half(core)], (((0,), (0,)), ((), ())), preferred_element_type=F32
        )
    state_ref[:HEAD_DIM] = state.astype(BF16)
    state_ref[HEAD_DIM:] = notes(last.astype(F32), count.astype(F32)).astype(BF16)


def notes(last, count):
    row = lax.broadcasted_iota(jnp.int32, (16, HEAD_DIM), 0)
    high = jnp.floor(count * (1.0 / 64.0))
    return jnp.where(
        row == 0, last, jnp.where(row == 1, high, jnp.where(row == 2, count - 64.0 * high, 0.0))
    )


def read_state(ref):
    tail = ref[HEAD_DIM:].astype(F32)
    return ref[:HEAD_DIM].astype(F32), tail[0:1], tail[1:2] * 64.0 + tail[2:3]


def plane_kernel(info, own, from1, from2, from3, prefix_ref, plane_ref):
    x = place()[1]
    first = info[3].astype(F32)
    items = [read_state(ref) for ref in (own, from1, from2, from3)]
    prefix = jnp.zeros((HEAD_DIM, HEAD_DIM), F32)
    prefix_count = jnp.zeros((1, HEAD_DIM), F32)
    for shift in (1, 2, 3):
        state, doc, count = items[shift]
        chosen = jnp.where((doc == first) & (x >= shift), 1.0, 0.0)
        prefix += state * chosen
        prefix_count += count * chosen
    prefix_ref[:HEAD_DIM] = prefix
    prefix_ref[HEAD_DIM:] = jnp.broadcast_to(prefix_count, (8, HEAD_DIM))
    last = items[0][1]
    for item in items[1:]:
        last = jnp.maximum(last, item[1])
    total = jnp.zeros((HEAD_DIM, HEAD_DIM), F32)
    total_count = jnp.zeros((1, HEAD_DIM), F32)
    for state, doc, count in items:
        chosen = jnp.where(doc == last, 1.0, 0.0)
        total += state * chosen
        total_count += count * chosen
    plane_ref[:HEAD_DIM] = total.astype(BF16)
    plane_ref[HEAD_DIM:] = notes(last, total_count).astype(BF16)


def document_start(info, rows):
    start = jnp.zeros_like(rows)
    for d in range(3):
        start = jnp.where(rows >= info[d], jnp.maximum(start, info[d]), start)
    return start


def split_dot(wide, narrow):
    high = wide.astype(BF16)
    low = (wide - high.astype(F32)).astype(BF16)
    return jnp.dot(high, narrow, preferred_element_type=F32) + jnp.dot(
        low, narrow, preferred_element_type=F32
    )


def inside_kernel(info, q1, q1_r, k1, k1_r, v1, v1_r, inside_ref, query_ref, keys, values):
    core = place()[2]
    mine, theirs = rows_of(core), rows_of(1 - core)
    own_cols = pl.ds(pl.multiple_of(core * COLS, COLS), COLS)
    query_ref[mine, :] = q1[:, own_cols]
    query_ref[theirs, :] = q1_r[:, own_cols]
    keys[mine, :] = k1[:, half(core)]
    keys[theirs, :] = k1_r[:, half(core)]
    values[mine, :] = v1[:, half(core)]
    values[theirs, :] = v1_r[:, half(core)]
    row = lax.broadcasted_iota(jnp.int32, (PAIR, PAIR), 0)
    column = lax.broadcasted_iota(jnp.int32, (PAIR, PAIR), 1)
    visible = (column <= row) & (column >= document_start(info, row))
    for head in range(REPEAT):
        cols = slice(head * HEAD_DIM, (head + 1) * HEAD_DIM)
        scores = lax.dot_general(
            query_ref[:, cols], keys[...], (((1,), (1,)), ((), ())), preferred_element_type=F32
        )
        scores = jnp.where(visible, scores, 0.0)
        inside_ref[:, cols] = split_dot(scores, values[...])


def row_sums(squares):
    high = squares.astype(BF16)
    low = (squares - high.astype(F32)).astype(BF16)
    ones = jnp.ones((8, squares.shape[1]), BF16)
    dims = (((1,), (1,)), ((), ()))
    return lax.dot_general(ones, high, dims, preferred_element_type=F32) + lax.dot_general(
        ones, low, dims, preferred_element_type=F32
    )


def first_kernel(
    info, prefix, from1, from2, from3, from4, inside, query, first_ref, sums_ref, count_ref
):
    z = place()[0]
    first = info[3].astype(F32)
    state = prefix[:HEAD_DIM]
    count = prefix[HEAD_DIM : HEAD_DIM + 1]
    for back, ref in enumerate((from1, from2, from3, from4), 1):
        one_state, doc, one_count = read_state(ref)
        chosen = jnp.where((doc == first) & (z >= back), 1.0, 0.0)
        state += one_state * chosen
        count += one_count * chosen
    count_ref[0] = jnp.max(count).astype(jnp.int32)
    high = state.astype(BF16)
    low = (state - high.astype(F32)).astype(BF16)
    in_first = lax.broadcasted_iota(jnp.int32, (PAIR, HEAD_DIM), 0) < info[6]
    squares = jnp.zeros((PAIR, HEAD_DIM), F32)
    for head in range(REPEAT):
        cols = slice(head * HEAD_DIM, (head + 1) * HEAD_DIM)
        queries = query[:, cols]
        earlier = jnp.dot(queries, high, preferred_element_type=F32) + jnp.dot(
            queries, low, preferred_element_type=F32
        )
        out = inside[:, cols] + jnp.where(in_first, earlier, 0.0)
        first_ref[:, cols] = out
        squares += out * out
    sums_ref[...] = row_sums(squares)


def row_scale(parts):
    total = parts[0][...]
    for part in parts[1:]:
        total = total + part[...]
    return lax.transpose(lax.rsqrt(total * (1.0 / WIDTH) + EPSILON), (1, 0))[:, :1]


def attention_kernel(*refs):
    info, reach, sum0, sum1, sum2, sum3, first, base, base_r = refs[:9]
    packs = refs[9 : 9 + 20]
    mine_ref, send_ref, mine_sums, send_sums = refs[29:33]
    kv, queries, tops, acc, scales, sems = refs[33:]
    _, x, core = place()
    prior = reach[0]
    low = PRIOR - prior
    chunk_first = low // CHUNK
    row_first = chunk_first * CHUNK

    def each_pack(act):
        for back in range(BACK + 1):
            for shift in range(X):
                if back == 0 and shift == 0:
                    distance = jnp.int32(0)
                else:
                    distance = 4 * back + shift - jnp.where(x < shift, 4, 0)
                start = (16 - distance) * PAIR
                needed = (distance >= 0) & (distance <= 16) & (start + PAIR > row_first)

                @pl.when(needed)
                def _():
                    at = pl.multiple_of(jnp.maximum(start, 0), PAIR)
                    act(
                        pltpu.make_async_copy(
                            packs[back * X + shift],
                            kv.at[pl.ds(at, PAIR), pl.ds(0, 2 * HEAD_DIM)],
                            sems.at[back * X + shift],
                        )
                    )

    each_pack(lambda copy: copy.start())
    kv[:, 2 * HEAD_DIM :] = jnp.ones((PRIOR + PAIR, HEAD_DIM), BF16)
    scales[...] = jnp.broadcast_to(row_scale((sum0, sum1, sum2, sum3)), (PAIR, HEAD_DIM))
    for part, where in ((base, rows_of(core)), (base_r, rows_of(1 - core))):
        for head in range(REPEAT):
            cols = pl.ds(pl.multiple_of(core * COLS + head * HEAD_DIM, HEAD_DIM), HEAD_DIM)
            value = part[:, cols].astype(F32) + (
                first[where, head * HEAD_DIM : (head + 1) * HEAD_DIM] * scales[where, :]
            )
            queries[head, where, :] = value.astype(BF16)
    tops[...] = jnp.full(tops.shape, NEGATIVE, F32)
    acc[...] = jnp.zeros(acc.shape, F32)
    each_pack(lambda copy: copy.wait())

    def absorb(head, start, length, visible):
        rows = pl.ds(start, length)
        scores = lax.dot_general(
            queries[head], kv[rows, :HEAD_DIM], (((1,), (1,)), ((), ())), preferred_element_type=F32
        )
        if visible is not None:
            scores = jnp.where(visible, scores, NEGATIVE)
        old_top = tops[head]
        top = jnp.maximum(old_top, jnp.max(scores, axis=1, keepdims=True))
        wide_top = jnp.concatenate([top] * (length // HEAD_DIM), axis=1)
        weights = jnp.exp2((scores - wide_top) * SCALE)
        if visible is not None:
            weights = jnp.where(visible, weights, 0.0)
        shrink = jnp.exp2((old_top - top) * SCALE)
        tops[head] = top
        acc[head] = acc[head] * jnp.concatenate([shrink, shrink], axis=1) + jnp.dot(
            weights.astype(BF16), kv[rows, HEAD_DIM:], preferred_element_type=F32
        )

    @pl.when(prior > 0)
    def _():
        column = lax.broadcasted_iota(jnp.int32, (PAIR, CHUNK), 1)
        visible = column >= low - row_first
        for head in range(REPEAT):
            absorb(head, pl.multiple_of(row_first, CHUNK), CHUNK, visible)

    @pl.loop(chunk_first + 1, PRIOR // CHUNK)
    def _(chunk):
        for head in range(REPEAT):
            absorb(head, pl.multiple_of(chunk * CHUNK, CHUNK), CHUNK, None)

    @pl.when(info[6] < PAIR)
    def _():
        in_first = lax.broadcasted_iota(jnp.int32, (PAIR, HEAD_DIM), 0) < info[6]
        for head in range(REPEAT):
            tops[head] = jnp.where(in_first, tops[head], NEGATIVE)
            acc[head] = jnp.where(jnp.concatenate([in_first, in_first], axis=1), acc[head], 0.0)

    row = lax.broadcasted_iota(jnp.int32, (PAIR, PAIR), 0)
    column = lax.broadcasted_iota(jnp.int32, (PAIR, PAIR), 1)
    visible = (column <= row) & (column >= document_start(info, row))
    for head in range(REPEAT):
        absorb(head, PRIOR, PAIR, visible)

    for out_ref, out_sums, where in (
        (mine_ref, mine_sums, rows_of(core)),
        (send_ref, send_sums, rows_of(1 - core)),
    ):
        squares = jnp.zeros((TOK, HEAD_DIM), F32)
        for head in range(REPEAT):
            summed = acc[head, where, :]
            out = (summed[:, :HEAD_DIM] / summed[:, HEAD_DIM:]).astype(BF16)
            out_ref[:, head * HEAD_DIM : (head + 1) * HEAD_DIM] = out
            widened = out.astype(F32)
            squares += widened * widened
        out_sums[...] = row_sums(squares)


def last_kernel(sum0, sum1, sum2, sum3, mine, theirs, out_ref):
    core = place()[2]
    scale = row_scale((sum0, sum1, sum2, sum3))
    for ref, side in ((mine, core), (theirs, 1 - core)):
        cols = pl.ds(pl.multiple_of(side * COLS, COLS), COLS)
        out_ref[:, cols] = (ref[...].astype(F32) * scale).astype(BF16)


def along(z_shift=0, x_shift=0, core_shift=0, keep=lambda z, x: True):
    pairs = []
    for z in range(Z):
        for x in range(X):
            for core in range(CORES):
                if keep(z, x):
                    to = ((z + z_shift) % Z * X + (x + x_shift) % X) * CORES
                    pairs.append(((z * X + x) * CORES + core, to + (core + core_shift) % CORES))
    return pairs


def swap(value):
    return lax.ppermute(value, "ctx", along(core_shift=1))


def over_tp(value):
    return [value] + [
        lax.ppermute(value, "tp", [(i, (i + shift) % TP) for i in range(TP)]) for shift in (1, 2, 3)
    ]


def shape(dims, kind):
    return jax.ShapeDtypeStruct(dims, kind)


def shards(query_one, key_one, value_one, segments, query_base, key_two, value_two):
    segments_r = swap(segments)
    k1_r, v1_r, k2_r, v2_r = swap(key_one), swap(value_one), swap(key_two), swap(value_two)
    q1_r, base_r = swap(query_one), swap(query_base)

    pack, state, info = call(
        prep_kernel,
        (shape((PAIR, 2 * HEAD_DIM), BF16), shape((144, HEAD_DIM), BF16), shape((8,), jnp.int32)),
        [SMEM, SMEM] + [VMEM] * 8,
        (VMEM, VMEM, SMEM),
        name="prep",
    )(segments, segments_r, key_one, k1_r, value_one, v1_r, key_two, k2_r, value_two, v2_r)

    columns = [pack]
    for back in range(BACK):
        columns.append(lax.ppermute(columns[-1], "ctx", along(z_shift=1)))
    packs = []
    for back in range(BACK + 1):
        packs.append(columns[back])
        for shift in (1, 2, 3):
            if back == 0:
                pairs = along(x_shift=shift, keep=lambda z, x: x + shift < X)
            elif back == BACK:
                pairs = along(x_shift=shift, keep=lambda z, x: x + shift >= X)
            else:
                pairs = along(x_shift=shift)
            packs.append(lax.ppermute(columns[back], "ctx", pairs))

    near = [lax.ppermute(state, "ctx", along(x_shift=shift)) for shift in (1, 2, 3)]
    prefix, plane = call(
        plane_kernel,
        (shape((HEAD_DIM + 8, HEAD_DIM), F32), shape((144, HEAD_DIM), BF16)),
        [SMEM] + [VMEM] * 4,
        (VMEM, VMEM),
        name="plane",
    )(info, state, *near)
    far = [lax.ppermute(plane, "ctx", along(z_shift=back)) for back in (1, 2, 3, 4)]

    inside, query = call(
        inside_kernel,
        (shape((PAIR, COLS), F32), shape((PAIR, COLS), BF16)),
        [SMEM] + [VMEM] * 6,
        (VMEM, VMEM),
        scratch=(pltpu.VMEM((PAIR, HEAD_DIM), BF16), pltpu.VMEM((PAIR, HEAD_DIM), BF16)),
        name="inside",
    )(info, query_one, q1_r, key_one, k1_r, value_one, v1_r)
    first, sums, reach = call(
        first_kernel,
        (shape((PAIR, COLS), F32), shape((8, PAIR), F32), shape((1,), jnp.int32)),
        [SMEM] + [VMEM] * 7,
        (VMEM, VMEM, SMEM),
        name="first",
    )(info, prefix, *far, inside, query)
    all_sums = over_tp(sums + swap(sums))

    mine, send, mine_sums, send_sums = call(
        attention_kernel,
        (
            shape((TOK, COLS), BF16),
            shape((TOK, COLS), BF16),
            shape((8, TOK), F32),
            shape((8, TOK), F32),
        ),
        [SMEM, SMEM] + [VMEM] * 7 + [ANY] * 20,
        (VMEM,) * 4,
        scratch=(
            pltpu.VMEM((PRIOR + PAIR, 3 * HEAD_DIM), BF16),
            pltpu.VMEM((REPEAT, PAIR, HEAD_DIM), BF16),
            pltpu.VMEM((REPEAT, PAIR, HEAD_DIM), F32),
            pltpu.VMEM((REPEAT, PAIR, 2 * HEAD_DIM), F32),
            pltpu.VMEM((PAIR, HEAD_DIM), F32),
            pltpu.SemaphoreType.DMA((20,)),
        ),
        limit=40 * 2**20,
        name="attention",
    )(info, reach, *all_sums, first, query_base, base_r, *packs)
    theirs = swap(send)
    out_sums = over_tp(mine_sums + swap(send_sums))
    return call(
        last_kernel, shape((TOK, 2 * COLS), BF16), [VMEM] * 6, VMEM, name="last"
    )(*out_sums, mine, theirs)


def solution(mesh):
    return jax.shard_map(
        shards,
        mesh=mesh,
        in_specs=(P("ctx", "tp"),) * 3 + (P("ctx"),) + (P("ctx", "tp"),) * 3,
        out_specs=P("ctx", "tp"),
        check_vma=False,
    )
```

time: 430 us -> 124 us (0.29)
  the two profiles are of different devices: /device:TPU:8 before, /device:TPU:128 now
where the time goes in v1:
time: 124 us; the launch traced here: 123 us
  starting transfers between devices  51.6 us (42%)
  waiting for transfers between devices  41.4 us (33%)
  Pallas kernels  24.2 us (20%)
  local copies, waits for them, and re-layouts  5.25 us (4%)
    ppermute x15, starting transfers between devices, shards(): packs.append(lax.ppermute(columns[back], 'ctx', pairs))  22.2 us
    ppermute x15, waiting for transfers between devices, shards(): packs.append(lax.ppermute(columns[back], 'ctx', pairs))  18.8 us
    pallas_call x1, Pallas kernels, shards(): call(attention_kernel, (shape((TOK, COLS), BF16), shape((TOK, COLS), BF16...  17.7 us
    ppermute x6, waiting for transfers between devices, over_tp(): lax.ppermute(value, 'tp', [(i, (i + shift) % TP) for i in range(TP)])  11.5 us
    ppermute x6, starting transfers between devices, over_tp(): lax.ppermute(value, 'tp', [(i, (i + shift) % TP) for i in range(TP)])  8.6 us
    ppermute x4, starting transfers between devices, shards(): lax.ppermute(plane, 'ctx', along(z_shift=back))  7.71 us
    ppermute x3, starting transfers between devices, shards(): lax.ppermute(state, 'ctx', along(x_shift=shift))  5.65 us
    ppermute x4, waiting for transfers between devices, shards(): lax.ppermute(plane, 'ctx', along(z_shift=back))  5.45 us
  transfers between devices with their start and end apart: 42, of which 22 were waited for; matrix products, arithmetic and copies ran while one was open for 0% of the time, Pallas kernels for 5%

profile of v1, /device:TPU:128, one launch (start us, length us, event | category | flops | bytes accessed | tf_op | source)
XLA Modules:
  0.0 122.7 jit_solution(14322311017704184136)
XLA Ops:
  11.7 2.7 %collective-permute-start.6 = (bf16[144,128]{1,0:T(8,128)(2,1)S(1)}, bf16[144,128]{1,0:T(8,128)(2,1)S(1)}, u32[]{:S(2)}, u32[]{:S(2)}) collective-permute-start(bf16[144,128]{1,0:T(8,128)(2,1)S(1)} %get-tuple-element.20.own), channel_id=1, source_target_pairs={{0,16},{4,20},{8,24},{12,28},{16,0},{20,4},{24,8},{28,12},{32,48},... | collective-permute-start | bytes 110600 | tf_op jit(solution)/shard_map/ppermute | solution.py:387
  20.0 4.5 %collective-permute-start.11 = (bf16[144,128]{1,0:T(8,128)(2,1)S(1)}, bf16[144,128]{1,0:T(8,128)(2,1)S(1)}, u32[]{:S(2)}, u32[]{:S(2)}) collective-permute-start(bf16[144,128]{1,0:T(8,128)(2,1)S(1)} %get-tuple-element.22), channel_id=1, source_target_pairs={{0,128},{4,132},{8,136},{12,140},{16,144},{20,148},{24,152},{28,15... | collective-permute-start | bytes 110600 | tf_op jit(solution)/shard_map/ppermute | solution.py:395
  29.7 2.2 %collective-permute-start.18 = (bf16[384,256]{1,0:T(8,128)(2,1)S(1)}, bf16[384,256]{1,0:T(8,128)(2,1)S(1)}, u32[]{:S(2)}, u32[]{:S(2)}) collective-permute-start(bf16[384,256]{1,0:T(8,128)(2,1)S(1)} %get-tuple-element.28.refs_9_), channel_id=1, source_target_pairs={{0,8},{4,12},{8,16},{12,20},{16,24},{20,28},{32,40},{36,44},{40,48... | collective-permute-start | bytes 589832 | tf_op jit(solution)/shard_map/ppermute | solution.py:385
  31.9 2.4 %collective-permute-done.9.from2 = bf16[144,128]{1,0:T(8,128)(2,1)S(1)} collective-permute-done((bf16[144,128]{1,0:T(8,128)(2,1)S(1)}, bf16[144,128]{1,0:T(8,128)(2,1)S(1)}, u32[]{:S(2)}, u32[]{:S(2)}) %collective-permute-start.9) | collective-permute-done | bytes 36896 | tf_op jit(solution)/shard_map/ppermute | solution.py:395
  34.3 3.4 %collective-permute-start.19 = (bf16[384,256]{1,0:T(8,128)(2,1)S(1)}, bf16[384,256]{1,0:T(8,128)(2,1)S(1)}, u32[]{:S(2)}, u32[]{:S(2)}) collective-permute-start(bf16[384,256]{1,0:T(8,128)(2,1)S(1)} %get-tuple-element.28.refs_9_), channel_id=1, source_target_pairs={{0,16},{4,20},{8,24},{12,28},{32,48},{36,52},{40,56},{44,60},{64,8... | collective-permute-start | bytes 589832 | tf_op jit(solution)/shard_map/ppermute | solution.py:385
  38.8 1.8 %collective-permute-start.20 = (bf16[384,256]{1,0:T(8,128)(2,1)S(1)}, bf16[384,256]{1,0:T(8,128)(2,1)S(1)}, u32[]{:S(2)}, u32[]{:S(2)}) collective-permute-start(bf16[384,256]{1,0:T(8,128)(2,1)S(1)} %get-tuple-element.28.refs_9_), channel_id=1, source_target_pairs={{0,24},{4,28},{32,56},{36,60},{64,88},{68,92},{96,120},{100,124},{... | collective-permute-start | bytes 589832 | tf_op jit(solution)/shard_map/ppermute | solution.py:385
  41.6 2.0 %inside.1 = (f32[384,512]{1,0:T(8,128)S(1)}, bf16[384,512]{1,0:T(8,128)(2,1)S(1)}) custom-call(s32[8]{0:T(128)S(1)} %get-tuple-element.19.info.refs_0_, bf16[192,1024]{1,0:T(8,128)(2,1)S(1)} %copy-done.5, bf16[192,1024]{1,0:T(8,128)(2,1)S(1)} %collective-permute-done.12.q1_r, bf16[192,256]{1,0:T(8,128)(2,1)S(1)} %copy-done.2, ...), custom_call_target="tpu_custom_call" | custom-call | tf_op jit(solution)/shard_map/inside/pallas_call | solution.py:397
  45.6 2.5 %collective-permute-start.29 = (bf16[384,256]{1,0:T(8,128)(2,1)S(1)}, bf16[384,256]{1,0:T(8,128)(2,1)S(1)}, u32[]{:S(2)}, u32[]{:S(2)}) collective-permute-start(bf16[384,256]{1,0:T(8,128)(2,1)S(1)} %collective-permute-done.25.refs_17_), channel_id=1, source_target_pairs={{0,32},{4,36},{8,40},{12,44},{16,48},{20,52},{24,56},{28,60},{32,6... | collective-permute-start | bytes 589832 | tf_op jit(solution)/shard_map/ppermute | solution.py:374
  48.2 3.2 %collective-permute-start.24 = (bf16[384,256]{1,0:T(8,128)(2,1)S(1)}, bf16[384,256]{1,0:T(8,128)(2,1)S(1)}, u32[]{:S(2)}, u32[]{:S(2)}) collective-permute-start(bf16[384,256]{1,0:T(8,128)(2,1)S(1)} %collective-permute-done.21.refs_13_), channel_id=1, source_target_pairs={{0,24},{4,28},{8,0},{12,4},{16,8},{20,12},{24,16},{28,20},{32,56},... | collective-permute-start | bytes 589832 | tf_op jit(solution)/shard_map/ppermute | solution.py:385
  53.0 3.3 %collective-permute-done.14.refs_3_ = f32[8,384]{1,0:T(8,128)S(1)} collective-permute-done((f32[8,384]{1,0:T(8,128)S(1)}, f32[8,384]{1,0:T(8,128)S(1)}, u32[]{:S(2)}, u32[]{:S(2)}) %collective-permute-start.14) | collective-permute-done | bytes 12320 | tf_op jit(solution)/shard_map/ppermute | solution.py:351
  56.3 2.0 %collective-permute-start.15 = (f32[8,384]{1,0:T(8,128)S(1)}, f32[8,384]{1,0:T(8,128)S(1)}, u32[]{:S(2)}, u32[]{:S(2)}) collective-permute-start(f32[8,384]{1,0:T(8,128)S(1)} %add.6.refs_2_), channel_id=1, source_target_pairs={{0,2},{1,3},{2,0},{3,1},{4,6},{5,7},{6,4},{7,5},{8,10},{9,11},{10,... | collective-permute-start | bytes 36872 | tf_op jit(solution)/shard_map/ppermute | solution.py:351
  58.3 3.2 %collective-permute-done.15.refs_4_ = f32[8,384]{1,0:T(8,128)S(1)} collective-permute-done((f32[8,384]{1,0:T(8,128)S(1)}, f32[8,384]{1,0:T(8,128)S(1)}, u32[]{:S(2)}, u32[]{:S(2)}) %collective-permute-start.15) | collective-permute-done | bytes 12320 | tf_op jit(solution)/shard_map/ppermute | solution.py:351
  61.5 1.8 %collective-permute-start.16 = (f32[8,384]{1,0:T(8,128)S(1)}, f32[8,384]{1,0:T(8,128)S(1)}, u32[]{:S(2)}, u32[]{:S(2)}) collective-permute-start(f32[8,384]{1,0:T(8,128)S(1)} %add.6.refs_2_), channel_id=1, source_target_pairs={{0,3},{1,0},{2,1},{3,2},{4,7},{5,4},{6,5},{7,6},{8,11},{9,8},{10,9... | collective-permute-start | bytes 36872 | tf_op jit(solution)/shard_map/ppermute | solution.py:351
  63.3 1.9 %collective-permute-done.16.refs_5_ = f32[8,384]{1,0:T(8,128)S(1)} collective-permute-done((f32[8,384]{1,0:T(8,128)S(1)}, f32[8,384]{1,0:T(8,128)S(1)}, u32[]{:S(2)}, u32[]{:S(2)}) %collective-permute-start.16) | collective-permute-done | bytes 12320 | tf_op jit(solution)/shard_map/ppermute | solution.py:351
  66.1 2.0 %collective-permute-start.27 = (bf16[384,256]{1,0:T(8,128)(2,1)S(1)}, bf16[384,256]{1,0:T(8,128)(2,1)S(1)}, u32[]{:S(2)}, u32[]{:S(2)}) collective-permute-start(bf16[384,256]{1,0:T(8,128)(2,1)S(1)} %collective-permute-done.25.refs_17_), channel_id=1, source_target_pairs={{0,16},{4,20},{8,24},{12,28},{16,0},{20,4},{24,8},{28,12},{32,48},... | collective-permute-start | bytes 589832 | tf_op jit(solution)/shard_map/ppermute | solution.py:385
  68.9 2.6 %collective-permute-start.28 = (bf16[384,256]{1,0:T(8,128)(2,1)S(1)}, bf16[384,256]{1,0:T(8,128)(2,1)S(1)}, u32[]{:S(2)}, u32[]{:S(2)}) collective-permute-start(bf16[384,256]{1,0:T(8,128)(2,1)S(1)} %collective-permute-done.25.refs_17_), channel_id=1, source_target_pairs={{0,24},{4,28},{8,0},{12,4},{16,8},{20,12},{24,16},{28,20},{32,56},... | collective-permute-start | bytes 589832 | tf_op jit(solution)/shard_map/ppermute | solution.py:385
  71.5 2.2 %collective-permute-done.26.refs_18_ = bf16[384,256]{1,0:T(8,128)(2,1)S(1)} collective-permute-done((bf16[384,256]{1,0:T(8,128)(2,1)S(1)}, bf16[384,256]{1,0:T(8,128)(2,1)S(1)}, u32[]{:S(2)}, u32[]{:S(2)}) %collective-permute-start.26) | collective-permute-done | bytes 196640 | tf_op jit(solution)/shard_map/ppermute | solution.py:385
  73.7 1.8 %collective-permute-start.31 = (bf16[384,256]{1,0:T(8,128)(2,1)S(1)}, bf16[384,256]{1,0:T(8,128)(2,1)S(1)}, u32[]{:S(2)}, u32[]{:S(2)}) collective-permute-start(bf16[384,256]{1,0:T(8,128)(2,1)S(1)} %collective-permute-done.29.refs_21_), channel_id=1, source_target_pairs={{0,16},{4,20},{8,24},{12,28},{16,0},{20,4},{24,8},{28,12},{32,48},... | collective-permute-start | bytes 589832 | tf_op jit(solution)/shard_map/ppermute | solution.py:385
  75.5 2.6 %collective-permute-done.27.refs_19_ = bf16[384,256]{1,0:T(8,128)(2,1)S(1)} collective-permute-done((bf16[384,256]{1,0:T(8,128)(2,1)S(1)}, bf16[384,256]{1,0:T(8,128)(2,1)S(1)}, u32[]{:S(2)}, u32[]{:S(2)}) %collective-permute-start.27) | collective-permute-done | bytes 196640 | tf_op jit(solution)/shard_map/ppermute | solution.py:385
  80.7 8.0 %collective-permute-done.30.refs_22_ = bf16[384,256]{1,0:T(8,128)(2,1)S(1)} collective-permute-done((bf16[384,256]{1,0:T(8,128)(2,1)S(1)}, bf16[384,256]{1,0:T(8,128)(2,1)S(1)}, u32[]{:S(2)}, u32[]{:S(2)}) %collective-permute-start.30) | collective-permute-done | bytes 196640 | tf_op jit(solution)/shard_map/ppermute | solution.py:385
  91.0 5.1 %collective-permute-done.36.refs_28_ = bf16[384,256]{1,0:T(8,128)(2,1)S(1)} collective-permute-done((bf16[384,256]{1,0:T(8,128)(2,1)S(1)}, bf16[384,256]{1,0:T(8,128)(2,1)S(1)}, u32[]{:S(2)}, u32[]{:S(2)}) %collective-permute-start.36) | collective-permute-done | bytes 196640 | tf_op jit(solution)/shard_map/ppermute | solution.py:385
  96.2 17.7 %attention.1 = (bf16[192,512]{1,0:T(8,128)(2,1)S(1)}, bf16[192,512]{1,0:T(8,128)(2,1)S(1)}, f32[8,192]{1,0:T(8,128)S(1)}, f32[8,192]{1,0:T(8,128)S(1)}) custom-call(s32[8]{0:T(128)S(1)} %get-tuple-element.19.info.refs_0_, s32[1]{0:T(128)} %get-tuple-element.25.refs_1_, f32[8,384]{1,0:T(8,128)S(1)} %add.6.refs_2_, ...), custom_call_target="tpu_custom_call" | custom-call | tf_op jit(solution)/shard_map/attention/pallas_call | solution.py:414
  115.5 2.6 %collective-permute-start.39 = (f32[8,192]{1,0:T(8,128)S(1)}, f32[8,192]{1,0:T(8,128)S(1)}, u32[]{:S(2)}, u32[]{:S(2)}) collective-permute-start(f32[8,192]{1,0:T(8,128)S(1)} %add.7.sum0), channel_id=1, source_target_pairs={{0,2},{1,3},{2,0},{3,1},{4,6},{5,7},{6,4},{7,5},{8,10},{9,11},{10,... | collective-permute-start | bytes 18440 | tf_op jit(solution)/shard_map/ppermute | solution.py:351
  118.7 1.6 %collective-permute-done.38.sum1 = f32[8,192]{1,0:T(8,128)S(1)} collective-permute-done((f32[8,192]{1,0:T(8,128)S(1)}, f32[8,192]{1,0:T(8,128)S(1)}, u32[]{:S(2)}, u32[]{:S(2)}) %collective-permute-start.38) | collective-permute-done | bytes 6176 | tf_op jit(solution)/shard_map/ppermute | solution.py:351
  (86 shorter events, 39.3 us)
Async XLA Ops:
  0.0 38.8 %collective-permute-start.12 = (bf16[192,1024]{1,0:T(8,128)(2,1)}, bf16[192,1024]{1,0:T(8,128)(2,1)S(1)}, u32[]{:S(2)}, u32[]{:S(2)}) collective-permute-start(bf16[192,1024]{1,0:T(8,128)(2,1)} %q1.1), channel_id=1, source_target_pairs={{0,4},{4,0},{8,12},{12,8},{16,20},{20,16},{24,28},{28,24},{32,36},... | collective-permute-start | bytes 1179656 | tf_op jit(solution)/shard_map/ppermute | solution.py:346
  9.1 28.7 %collective-permute-start.21 = (bf16[384,256]{1,0:T(8,128)(2,1)S(1)}, bf16[384,256]{1,0:T(8,128)(2,1)S(1)}, u32[]{:S(2)}, u32[]{:S(2)}) collective-permute-start(bf16[384,256]{1,0:T(8,128)(2,1)S(1)} %get-tuple-element.28.refs_9_), channel_id=1, source_target_pairs={{0,32},{4,36},{8,40},{12,44},{16,48},{20,52},{24,56},{28,60},{32,6... | collective-permute-start | bytes 589832 | tf_op jit(solution)/shard_map/ppermute | solution.py:374
  18.9 7.8 %collective-permute-start.10 = (bf16[144,128]{1,0:T(8,128)(2,1)S(1)}, bf16[144,128]{1,0:T(8,128)(2,1)S(1)}, u32[]{:S(2)}, u32[]{:S(2)}) collective-permute-start(bf16[144,128]{1,0:T(8,128)(2,1)S(1)} %get-tuple-element.22), channel_id=1, source_target_pairs={{0,96},{4,100},{8,104},{12,108},{16,112},{20,116},{24,120},{28,124... | collective-permute-start | bytes 110600 | tf_op jit(solution)/shard_map/ppermute | solution.py:395
  20.0 8.2 %collective-permute-start.11 = (bf16[144,128]{1,0:T(8,128)(2,1)S(1)}, bf16[144,128]{1,0:T(8,128)(2,1)S(1)}, u32[]{:S(2)}, u32[]{:S(2)}) collective-permute-start(bf16[144,128]{1,0:T(8,128)(2,1)S(1)} %get-tuple-element.22), channel_id=1, source_target_pairs={{0,128},{4,132},{8,136},{12,140},{16,144},{20,148},{24,152},{28,15... | collective-permute-start | bytes 110600 | tf_op jit(solution)/shard_map/ppermute | solution.py:395
  26.7 24.7 %collective-permute-start.17 = (bf16[192,1024]{1,0:T(8,128)(2,1)S(1)}, bf16[192,1024]{1,0:T(8,128)(2,1)S(1)}, u32[]{:S(2)}, u32[]{:S(2)}) collective-permute-start(bf16[192,1024]{1,0:T(8,128)(2,1)S(1)} %copy-done), channel_id=1, source_target_pairs={{0,4},{4,0},{8,12},{12,8},{16,20},{20,16},{24,28},{28,24},{32,36},... | collective-permute-start | bytes 1179656 | tf_op jit(solution)/shard_map/ppermute | solution.py:346
  29.7 15.5 %collective-permute-start.18 = (bf16[384,256]{1,0:T(8,128)(2,1)S(1)}, bf16[384,256]{1,0:T(8,128)(2,1)S(1)}, u32[]{:S(2)}, u32[]{:S(2)}) collective-permute-start(bf16[384,256]{1,0:T(8,128)(2,1)S(1)} %get-tuple-element.28.refs_9_), channel_id=1, source_target_pairs={{0,8},{4,12},{8,16},{12,20},{16,24},{20,28},{32,40},{36,44},{40,48... | collective-permute-start | bytes 589832 | tf_op jit(solution)/shard_map/ppermute | solution.py:385
  34.3 11.0 %collective-permute-start.19 = (bf16[384,256]{1,0:T(8,128)(2,1)S(1)}, bf16[384,256]{1,0:T(8,128)(2,1)S(1)}, u32[]{:S(2)}, u32[]{:S(2)}) collective-permute-start(bf16[384,256]{1,0:T(8,128)(2,1)S(1)} %get-tuple-element.28.refs_9_), channel_id=1, source_target_pairs={{0,16},{4,20},{8,24},{12,28},{32,48},{36,52},{40,56},{44,60},{64,8... | collective-permute-start | bytes 589832 | tf_op jit(solution)/shard_map/ppermute | solution.py:385
  37.8 7.9 %collective-permute-start.25 = (bf16[384,256]{1,0:T(8,128)(2,1)S(1)}, bf16[384,256]{1,0:T(8,128)(2,1)S(1)}, u32[]{:S(2)}, u32[]{:S(2)}) collective-permute-start(bf16[384,256]{1,0:T(8,128)(2,1)S(1)} %collective-permute-done.21.refs_13_), channel_id=1, source_target_pairs={{0,32},{4,36},{8,40},{12,44},{16,48},{20,52},{24,56},{28,60},{32,6... | collective-permute-start | bytes 589832 | tf_op jit(solution)/shard_map/ppermute | solution.py:374
  38.8 9.4 %collective-permute-start.20 = (bf16[384,256]{1,0:T(8,128)(2,1)S(1)}, bf16[384,256]{1,0:T(8,128)(2,1)S(1)}, u32[]{:S(2)}, u32[]{:S(2)}) collective-permute-start(bf16[384,256]{1,0:T(8,128)(2,1)S(1)} %get-tuple-element.28.refs_9_), channel_id=1, source_target_pairs={{0,24},{4,28},{32,56},{36,60},{64,88},{68,92},{96,120},{100,124},{... | collective-permute-start | bytes 589832 | tf_op jit(solution)/shard_map/ppermute | solution.py:385
  45.3 20.7 %collective-permute-start.22 = (bf16[384,256]{1,0:T(8,128)(2,1)S(1)}, bf16[384,256]{1,0:T(8,128)(2,1)S(1)}, u32[]{:S(2)}, u32[]{:S(2)}) collective-permute-start(bf16[384,256]{1,0:T(8,128)(2,1)S(1)} %collective-permute-done.21.refs_13_), channel_id=1, source_target_pairs={{0,8},{4,12},{8,16},{12,20},{16,24},{20,28},{24,0},{28,4},{32,40},... | collective-permute-start | bytes 589832 | tf_op jit(solution)/shard_map/ppermute | solution.py:385
  45.6 22.4 %collective-permute-start.29 = (bf16[384,256]{1,0:T(8,128)(2,1)S(1)}, bf16[384,256]{1,0:T(8,128)(2,1)S(1)}, u32[]{:S(2)}, u32[]{:S(2)}) collective-permute-start(bf16[384,256]{1,0:T(8,128)(2,1)S(1)} %collective-permute-done.25.refs_17_), channel_id=1, source_target_pairs={{0,32},{4,36},{8,40},{12,44},{16,48},{20,52},{24,56},{28,60},{32,6... | collective-permute-start | bytes 589832 | tf_op jit(solution)/shard_map/ppermute | solution.py:374
  48.2 20.7 %collective-permute-start.23 = (bf16[384,256]{1,0:T(8,128)(2,1)S(1)}, bf16[384,256]{1,0:T(8,128)(2,1)S(1)}, u32[]{:S(2)}, u32[]{:S(2)}) collective-permute-start(bf16[384,256]{1,0:T(8,128)(2,1)S(1)} %collective-permute-done.21.refs_13_), channel_id=1, source_target_pairs={{0,16},{4,20},{8,24},{12,28},{16,0},{20,4},{24,8},{28,12},{32,48},... | collective-permute-start | bytes 589832 | tf_op jit(solution)/shard_map/ppermute | solution.py:385
  48.2 23.3 %collective-permute-start.24 = (bf16[384,256]{1,0:T(8,128)(2,1)S(1)}, bf16[384,256]{1,0:T(8,128)(2,1)S(1)}, u32[]{:S(2)}, u32[]{:S(2)}) collective-permute-start(bf16[384,256]{1,0:T(8,128)(2,1)S(1)} %collective-permute-done.21.refs_13_), channel_id=1, source_target_pairs={{0,24},{4,28},{8,0},{12,4},{16,8},{20,12},{24,16},{28,20},{32,56},... | collective-permute-start | bytes 589832 | tf_op jit(solution)/shard_map/ppermute | solution.py:385
  65.2 8.5 %collective-permute-start.26 = (bf16[384,256]{1,0:T(8,128)(2,1)S(1)}, bf16[384,256]{1,0:T(8,128)(2,1)S(1)}, u32[]{:S(2)}, u32[]{:S(2)}) collective-permute-start(bf16[384,256]{1,0:T(8,128)(2,1)S(1)} %collective-permute-done.25.refs_17_), channel_id=1, source_target_pairs={{0,8},{4,12},{8,16},{12,20},{16,24},{20,28},{24,0},{28,4},{32,40},... | collective-permute-start | bytes 589832 | tf_op jit(solution)/shard_map/ppermute | solution.py:385
  66.1 12.0 %collective-permute-start.27 = (bf16[384,256]{1,0:T(8,128)(2,1)S(1)}, bf16[384,256]{1,0:T(8,128)(2,1)S(1)}, u32[]{:S(2)}, u32[]{:S(2)}) collective-permute-start(bf16[384,256]{1,0:T(8,128)(2,1)S(1)} %collective-permute-done.25.refs_17_), channel_id=1, source_target_pairs={{0,16},{4,20},{8,24},{12,28},{16,0},{20,4},{24,8},{28,12},{32,48},... | collective-permute-start | bytes 589832 | tf_op jit(solution)/shard_map/ppermute | solution.py:385
  68.1 10.0 %collective-permute-start.33 = (bf16[384,256]{1,0:T(8,128)(2,1)S(1)}, bf16[384,256]{1,0:T(8,128)(2,1)S(1)}, u32[]{:S(2)}, u32[]{:S(2)}) collective-permute-start(bf16[384,256]{1,0:T(8,128)(2,1)S(1)} %collective-permute-done.29.refs_21_), channel_id=1, source_target_pairs={{0,32},{4,36},{8,40},{12,44},{16,48},{20,52},{24,56},{28,60},{32,6... | collective-permute-start | bytes 589832 | tf_op jit(solution)/shard_map/ppermute | solution.py:374
  68.9 10.5 %collective-permute-start.28 = (bf16[384,256]{1,0:T(8,128)(2,1)S(1)}, bf16[384,256]{1,0:T(8,128)(2,1)S(1)}, u32[]{:S(2)}, u32[]{:S(2)}) collective-permute-start(bf16[384,256]{1,0:T(8,128)(2,1)S(1)} %collective-permute-done.25.refs_17_), channel_id=1, source_target_pairs={{0,24},{4,28},{8,0},{12,4},{16,8},{20,12},{24,16},{28,20},{32,56},... | collective-permute-start | bytes 589832 | tf_op jit(solution)/shard_map/ppermute | solution.py:385
  71.5 17.1 %collective-permute-start.30 = (bf16[384,256]{1,0:T(8,128)(2,1)S(1)}, bf16[384,256]{1,0:T(8,128)(2,1)S(1)}, u32[]{:S(2)}, u32[]{:S(2)}) collective-permute-start(bf16[384,256]{1,0:T(8,128)(2,1)S(1)} %collective-permute-done.29.refs_21_), channel_id=1, source_target_pairs={{0,8},{4,12},{8,16},{12,20},{16,24},{20,28},{24,0},{28,4},{32,40},... | collective-permute-start | bytes 589832 | tf_op jit(solution)/shard_map/ppermute | solution.py:385
  73.7 16.4 %collective-permute-start.31 = (bf16[384,256]{1,0:T(8,128)(2,1)S(1)}, bf16[384,256]{1,0:T(8,128)(2,1)S(1)}, u32[]{:S(2)}, u32[]{:S(2)}) collective-permute-start(bf16[384,256]{1,0:T(8,128)(2,1)S(1)} %collective-permute-done.29.refs_21_), channel_id=1, source_target_pairs={{0,16},{4,20},{8,24},{12,28},{16,0},{20,4},{24,8},{28,12},{32,48},... | collective-permute-start | bytes 589832 | tf_op jit(solution)/shard_map/ppermute | solution.py:385
  78.0 12.1 %collective-permute-start.32 = (bf16[384,256]{1,0:T(8,128)(2,1)S(1)}, bf16[384,256]{1,0:T(8,128)(2,1)S(1)}, u32[]{:S(2)}, u32[]{:S(2)}) collective-permute-start(bf16[384,256]{1,0:T(8,128)(2,1)S(1)} %collective-permute-done.29.refs_21_), channel_id=1, source_target_pairs={{0,24},{4,28},{8,0},{12,4},{16,8},{20,12},{24,16},{28,20},{32,56},... | collective-permute-start | bytes 589832 | tf_op jit(solution)/shard_map/ppermute | solution.py:385
  78.0 13.0 %collective-permute-start.34 = (bf16[384,256]{1,0:T(8,128)(2,1)S(1)}, bf16[384,256]{1,0:T(8,128)(2,1)S(1)}, u32[]{:S(2)}, u32[]{:S(2)}) collective-permute-start(bf16[384,256]{1,0:T(8,128)(2,1)S(1)} %collective-permute-done.33.refs_25_), channel_id=1, source_target_pairs={{24,0},{28,4},{56,32},{60,36},{88,64},{92,68},{120,96},{124,100},{... | collective-permute-start | bytes 589832 | tf_op jit(solution)/shard_map/ppermute | solution.py:385
  79.4 11.7 %collective-permute-start.35 = (bf16[384,256]{1,0:T(8,128)(2,1)S(1)}, bf16[384,256]{1,0:T(8,128)(2,1)S(1)}, u32[]{:S(2)}, u32[]{:S(2)}) collective-permute-start(bf16[384,256]{1,0:T(8,128)(2,1)S(1)} %collective-permute-done.33.refs_25_), channel_id=1, source_target_pairs={{16,0},{20,4},{24,8},{28,12},{48,32},{52,36},{56,40},{60,44},{80,6... | collective-permute-start | bytes 589832 | tf_op jit(solution)/shard_map/ppermute | solution.py:385
  88.6 7.6 %collective-permute-start.36 = (bf16[384,256]{1,0:T(8,128)(2,1)S(1)}, bf16[384,256]{1,0:T(8,128)(2,1)S(1)}, u32[]{:S(2)}, u32[]{:S(2)}) collective-permute-start(bf16[384,256]{1,0:T(8,128)(2,1)S(1)} %collective-permute-done.33.refs_25_), channel_id=1, source_target_pairs={{8,0},{12,4},{16,8},{20,12},{24,16},{28,20},{40,32},{44,36},{48,40... | collective-permute-start | bytes 589832 | tf_op jit(solution)/shard_map/ppermute | solution.py:385
  113.9 7.8 %collective-permute-start.41 = (bf16[192,512]{1,0:T(8,128)(2,1)S(1)}, bf16[192,512]{1,0:T(8,128)(2,1)S(1)}, u32[]{:S(2)}, u32[]{:S(2)}) collective-permute-start(bf16[192,512]{1,0:T(8,128)(2,1)S(1)} %get-tuple-element.32), channel_id=1, source_target_pairs={{0,4},{4,0},{8,12},{12,8},{16,20},{20,16},{24,28},{28,24},{32,36},... | collective-permute-start | bytes 589832 | tf_op jit(solution)/shard_map/ppermute | solution.py:346
  (27 other events, 162.7 us)

commit v2 on v1

v2 whole, which is shorter than its diff:
```python
import jax
import jax.numpy as jnp
from jax import lax
from jax.experimental import pallas as pl
from jax.experimental.pallas import tpu as pltpu
from jax.sharding import Mesh, PartitionSpec as P

HEAD_DIM = 128
WIDTH = 4096
EPSILON = 1e-05
NEGATIVE = -1e30

TOK = 192
PAIR = 384
REPEAT = 4
COLS = REPEAT * HEAD_DIM
Z, X, CORES, TP = 8, 4, 2, 4
BACK = 4
PRIOR = 16 * PAIR
CHUNK = 1536
SCALE = HEAD_DIM ** (-0.5) * 1.4426950408889634

F32 = jnp.float32
BF16 = jnp.bfloat16
VMEM = pl.BlockSpec(memory_space=pltpu.VMEM)
SMEM = pl.BlockSpec(memory_space=pltpu.SMEM)
ANY = pl.BlockSpec(memory_space=pl.ANY)


def place():
    return lax.axis_index("z"), lax.axis_index("x"), lax.axis_index("core")


def call(kernel, outs, specs_in, specs_out, scratch=(), limit=None, name=None):
    return pl.pallas_call(
        kernel,
        out_shape=outs,
        in_specs=specs_in,
        out_specs=specs_out,
        scratch_shapes=list(scratch),
        compiler_params=pltpu.CompilerParams(vmem_limit_bytes=limit or 16 * 2**20),
        name=name,
    )


def count_below(ref, doc):
    found = jnp.int32(0)
    for step in (128, 64, 32, 16, 8, 4, 2, 1):
        tried = found + step
        last = ref[jnp.minimum(tried, TOK) - 1]
        found = jnp.where((tried <= TOK) & (last < doc), tried, found)
    return found


def half(core):
    return pl.ds(pl.multiple_of(core * HEAD_DIM, HEAD_DIM), HEAD_DIM)


def rows_of(core):
    return pl.ds(pl.multiple_of(core * TOK, 64), TOK)


def prep_kernel(
    seg_any, seg_r, k1_any, k1_r, v1_any, v1_r, k2_any, k2_r, v2_any, v2_r, q1_any, base_any,
    pack_ref, state_ref, query_ref, info_ref, seg, k1, v1, sems
):
    core = place()[2]
    mine, theirs = rows_of(core), rows_of(1 - core)
    other_cols = pl.ds(pl.multiple_of((1 - core) * COLS, COLS), COLS)
    copies = [
        pltpu.make_async_copy(source, to, sems.at[at])
        for at, (source, to) in enumerate(
            (
                (seg_any, seg),
                (k1_any.at[:, half(core)], k1),
                (v1_any.at[:, half(core)], v1),
                (k2_any.at[:, half(core)], pack_ref.at[mine, pl.ds(0, HEAD_DIM)]),
                (v2_any.at[:, half(core)], pack_ref.at[mine, pl.ds(HEAD_DIM, HEAD_DIM)]),
                (q1_any.at[:, other_cols], query_ref.at[0]),
                (base_any.at[:, other_cols], query_ref.at[1]),
            )
        )
    ]
    for copy in copies:
        copy.start()
    pack_ref[theirs, :HEAD_DIM] = k2_r[:, half(core)]
    pack_ref[theirs, HEAD_DIM:] = v2_r[:, half(core)]
    for copy in copies:
        copy.wait()
    below = [count_below(seg, d) for d in (1, 2, 3)]
    below_r = [count_below(seg_r, d) for d in (1, 2, 3)]
    bounds = [a + b for a, b in zip(below, below_r)]
    first = jnp.where(core == 0, seg[0], seg_r[0])
    last = jnp.where(core == 0, seg_r[TOK - 1], seg[TOK - 1])

    def pick(values, doc):
        out = jnp.int32(0)
        for d in (1, 2, 3):
            out = jnp.where(doc == d, values[d - 1], out)
        return out

    count = PAIR - pick(bounds, last)
    first_end = jnp.where(first == 3, PAIR, pick(bounds, first + 1))
    for place_in, value in enumerate((*bounds, first, last, count, first_end, 0)):
        info_ref[place_in] = jnp.int32(value)
    rows = lax.broadcasted_iota(jnp.int32, (TOK, HEAD_DIM), 0)
    state = jnp.zeros((HEAD_DIM, HEAD_DIM), F32)
    for keys, values, start in (
        (k1[...], v1[...], pick(below, last)),
        (k1_r[:, half(core)], v1_r[:, half(core)], pick(below_r, last)),
    ):
        masked = jnp.where(rows >= start, keys.astype(F32), 0.0).astype(BF16)
        state += lax.dot_general(
            masked, values, (((0,), (0,)), ((), ())), preferred_element_type=F32
        )
    state_ref[:HEAD_DIM] = state.astype(BF16)
    state_ref[HEAD_DIM:] = notes(last.astype(F32), count.astype(F32)).astype(BF16)


def notes(last, count):
    row = lax.broadcasted_iota(jnp.int32, (16, HEAD_DIM), 0)
    high = jnp.floor(count * (1.0 / 64.0))
    return jnp.where(
        row == 0, last, jnp.where(row == 1, high, jnp.where(row == 2, count - 64.0 * high, 0.0))
    )


def read_state(ref):
    tail = ref[HEAD_DIM:].astype(F32)
    return ref[:HEAD_DIM].astype(F32), tail[0:1], tail[1:2] * 64.0 + tail[2:3]


def plane_kernel(info, own, from1, from2, from3, prefix_ref, plane_ref):
    x = place()[1]
    first = info[3].astype(F32)
    items = [read_state(ref) for ref in (own, from1, from2, from3)]
    prefix = jnp.zeros((HEAD_DIM, HEAD_DIM), F32)
    prefix_count = jnp.zeros((1, HEAD_DIM), F32)
    for shift in (1, 2, 3):
        state, doc, count = items[shift]
        chosen = jnp.where((doc == first) & (x >= shift), 1.0, 0.0)
        prefix += state * chosen
        prefix_count += count * chosen
    prefix_ref[:HEAD_DIM] = prefix
    prefix_ref[HEAD_DIM:] = jnp.broadcast_to(prefix_count, (8, HEAD_DIM))
    last = items[0][1]
    for item in items[1:]:
        last = jnp.maximum(last, item[1])
    total = jnp.zeros((HEAD_DIM, HEAD_DIM), F32)
    total_count = jnp.zeros((1, HEAD_DIM), F32)
    for state, doc, count in items:
        chosen = jnp.where(doc == last, 1.0, 0.0)
        total += state * chosen
        total_count += count * chosen
    plane_ref[:HEAD_DIM] = total.astype(BF16)
    plane_ref[HEAD_DIM:] = notes(last, total_count).astype(BF16)


def document_start(info, rows):
    start = jnp.zeros_like(rows)
    for d in range(3):
        start = jnp.where(rows >= info[d], jnp.maximum(start, info[d]), start)
    return start


def split_dot(wide, narrow):
    high = wide.astype(BF16)
    low = (wide - high.astype(F32)).astype(BF16)
    return jnp.dot(high, narrow, preferred_element_type=F32) + jnp.dot(
        low, narrow, preferred_element_type=F32
    )


def inside_kernel(
    info, q1_any, queries_r, k1_any, k1_r, v1_any, v1_r, inside_ref, query_ref, keys, values, sems
):
    core = place()[2]
    mine, theirs = rows_of(core), rows_of(1 - core)
    own_cols = pl.ds(pl.multiple_of(core * COLS, COLS), COLS)
    copies = [
        pltpu.make_async_copy(source, to, sems.at[at])
        for at, (source, to) in enumerate(
            (
                (q1_any.at[:, own_cols], query_ref.at[mine, :]),
                (k1_any.at[:, half(core)], keys.at[mine, :]),
                (v1_any.at[:, half(core)], values.at[mine, :]),
            )
        )
    ]
    for copy in copies:
        copy.start()
    query_ref[theirs, :] = queries_r[0]
    keys[theirs, :] = k1_r[:, half(core)]
    values[theirs, :] = v1_r[:, half(core)]
    for copy in copies:
        copy.wait()
    row = lax.broadcasted_iota(jnp.int32, (PAIR, PAIR), 0)
    column = lax.broadcasted_iota(jnp.int32, (PAIR, PAIR), 1)
    visible = (column <= row) & (column >= document_start(info, row))
    for head in range(REPEAT):
        cols = slice(head * HEAD_DIM, (head + 1) * HEAD_DIM)
        scores = lax.dot_general(
            query_ref[:, cols], keys[...], (((1,), (1,)), ((), ())), preferred_element_type=F32
        )
        scores = jnp.where(visible, scores, 0.0)
        inside_ref[:, cols] = split_dot(scores, values[...])


def row_sums(squares):
    high = squares.astype(BF16)
    low = (squares - high.astype(F32)).astype(BF16)
    ones = jnp.ones((8, squares.shape[1]), BF16)
    dims = (((1,), (1,)), ((), ()))
    return lax.dot_general(ones, high, dims, preferred_element_type=F32) + lax.dot_general(
        ones, low, dims, preferred_element_type=F32
    )


def first_kernel(
    info, prefix, from1, from2, from3, from4, inside, query, first_ref, sums_ref, count_ref
):
    z = place()[0]
    first = info[3].astype(F32)
    state = prefix[:HEAD_DIM]
    count = prefix[HEAD_DIM : HEAD_DIM + 1]
    for back, ref in enumerate((from1, from2, from3, from4), 1):
        one_state, doc, one_count = read_state(ref)
        chosen = jnp.where((doc == first) & (z >= back), 1.0, 0.0)
        state += one_state * chosen
        count += one_count * chosen
    count_ref[0] = jnp.max(count).astype(jnp.int32)
    high = state.astype(BF16)
    low = (state - high.astype(F32)).astype(BF16)
    in_first = lax.broadcasted_iota(jnp.int32, (PAIR, HEAD_DIM), 0) < info[6]
    squares = jnp.zeros((PAIR, HEAD_DIM), F32)
    for head in range(REPEAT):
        cols = slice(head * HEAD_DIM, (head + 1) * HEAD_DIM)
        queries = query[:, cols]
        earlier = jnp.dot(queries, high, preferred_element_type=F32) + jnp.dot(
            queries, low, preferred_element_type=F32
        )
        out = inside[:, cols] + jnp.where(in_first, earlier, 0.0)
        first_ref[:, cols] = out
        squares += out * out
    sums = row_sums(squares)
    for to in range(CORES * TP):
        sums_ref[to] = sums


def row_scale(sums):
    total = sums[0]
    for device in range(1, CORES * TP):
        total = total + sums[device]
    return lax.transpose(lax.rsqrt(total * (1.0 / WIDTH) + EPSILON), (1, 0))[:, :1]


TILE = 128
TILES = [(head, slice(at, at + TILE)) for head in range(REPEAT) for at in range(0, PAIR, TILE)]


def attention_kernel(
    info, reach, sums, first, base_any, queries_r, own0, own1, own23, own4, *refs
):
    gathered = refs[:9]
    mine_ref, send_ref, sums_ref = refs[9:12]
    kv, queries, tops, acc, scales, base, sems = refs[12:]
    _, x, core = place()
    own_cols = pl.ds(pl.multiple_of(core * COLS, COLS), COLS)
    base_copy = pltpu.make_async_copy(base_any.at[:, own_cols], base, sems.at[20])
    base_copy.start()
    prior = reach[0]
    low = PRIOR - prior
    chunk_first = low // CHUNK
    row_first = chunk_first * CHUNK

    upper, lower = pl.ds(0, PAIR), pl.ds(PAIR, PAIR)
    packs = [(own0, 0), (own1, 4), (own23.at[upper], 8), (own23.at[lower], 12), (own4, 16)]
    for shift in (1, 2, 3):
        wrapped = jnp.where(x < shift, 4, 0)
        packs.append((gathered[shift - 1], 4 + shift - wrapped))
        packs.append((gathered[shift + 2], shift + 3 * wrapped))
        packs.append((gathered[shift + 5].at[upper], 8 + shift - wrapped))
        packs.append((gathered[shift + 5].at[lower], 12 + shift - wrapped))

    def each_pack(act):
        for at, (ref, distance) in enumerate(packs):
            start = (16 - jnp.int32(distance)) * PAIR

            @pl.when(start + PAIR > row_first)
            def _():
                rows = pl.ds(pl.multiple_of(start, PAIR), PAIR)
                act(pltpu.make_async_copy(ref, kv.at[rows, pl.ds(0, 2 * HEAD_DIM)], sems.at[at]))

    each_pack(lambda copy: copy.start())
    kv[:, 2 * HEAD_DIM :] = jnp.ones((PRIOR + PAIR, HEAD_DIM), BF16)
    scales[...] = jnp.broadcast_to(row_scale(sums), (PAIR, HEAD_DIM))
    tops[...] = jnp.full(tops.shape, NEGATIVE, F32)
    acc[...] = jnp.zeros(acc.shape, F32)
    base_copy.wait()
    for part, where in ((base, rows_of(core)), (queries_r.at[1], rows_of(1 - core))):
        for head in range(REPEAT):
            cols = slice(head * HEAD_DIM, (head + 1) * HEAD_DIM)
            value = part[:, cols].astype(F32) + first[where, cols] * scales[where, :]
            queries[head, where, :] = value.astype(BF16)
    each_pack(lambda copy: copy.wait())

    def scores_of(head, part, rows):
        return lax.dot_general(
            queries[head, part],
            kv[rows, :HEAD_DIM],
            (((1,), (1,)), ((), ())),
            preferred_element_type=F32,
        )

    def update(head, part, scores, rows, visible):
        if visible is not None:
            scores = jnp.where(visible, scores, NEGATIVE)
        old_top = tops[head, part]
        top = jnp.maximum(old_top, jnp.max(scores, axis=1, keepdims=True))
        wide_top = jnp.concatenate([top] * (scores.shape[1] // HEAD_DIM), axis=1)
        weights = jnp.exp2((scores - wide_top) * SCALE)
        if visible is not None:
            weights = jnp.where(visible, weights, 0.0)
        shrink = jnp.exp2((old_top - top) * SCALE)
        tops[head, part] = top
        acc[head, part] = acc[head, part] * jnp.concatenate([shrink, shrink], axis=1) + jnp.dot(
            weights.astype(BF16), kv[rows, HEAD_DIM:], preferred_element_type=F32
        )

    def sweep(start, length, visible):
        rows = pl.ds(start, length)
        ahead = scores_of(*TILES[0], rows)
        for at, (head, part) in enumerate(TILES):
            scores = ahead
            if at + 1 < len(TILES):
                ahead = scores_of(*TILES[at + 1], rows)
            update(head, part, scores, rows, None if visible is None else visible(part))

    @pl.when(prior > 0)
    def _():
        column = lax.broadcasted_iota(jnp.int32, (TILE, CHUNK), 1)
        sweep(pl.multiple_of(row_first, CHUNK), CHUNK, lambda part: column >= low - row_first)

    @pl.loop(chunk_first + 1, PRIOR // CHUNK)
    def _(chunk):
        sweep(pl.multiple_of(chunk * CHUNK, CHUNK), CHUNK, None)

    @pl.when(info[6] < PAIR)
    def _():
        in_first = lax.broadcasted_iota(jnp.int32, (PAIR, HEAD_DIM), 0) < info[6]
        for head in range(REPEAT):
            tops[head] = jnp.where(in_first, tops[head], NEGATIVE)
            acc[head] = jnp.where(jnp.concatenate([in_first, in_first], axis=1), acc[head], 0.0)

    def own_visible(part):
        row = lax.broadcasted_iota(jnp.int32, (TILE, PAIR), 0) + part.start
        column = lax.broadcasted_iota(jnp.int32, (TILE, PAIR), 1)
        return (column <= row) & (column >= document_start(info, row))

    sweep(PRIOR, PAIR, own_visible)

    for side in range(CORES):
        where = slice(side * TOK, (side + 1) * TOK)
        squares = jnp.zeros((TOK, HEAD_DIM), F32)
        outs = []
        for head in range(REPEAT):
            summed = acc[head, where, :]
            out = (summed[:, :HEAD_DIM] / summed[:, HEAD_DIM:]).astype(BF16)
            outs.append(out)
            widened = out.astype(F32)
            squares += widened * widened
        whole = jnp.concatenate(outs, axis=1)

        @pl.when(core == side)
        def _():
            mine_ref[...] = whole

        @pl.when(core != side)
        def _():
            send_ref[...] = whole

        sums = row_sums(squares)
        for to in range(TP):
            sums_ref[side * TP + to] = sums


def last_kernel(sums, mine, theirs, out_ref):
    core = place()[2]
    scale = row_scale(sums)
    for ref, side in ((mine, core), (theirs, 1 - core)):
        cols = pl.ds(pl.multiple_of(side * COLS, COLS), COLS)
        out_ref[:, cols] = (ref[...].astype(F32) * scale).astype(BF16)


CTX = ("z", "x", "core")


def move(value, z_shift=0, x_shift=0, core_shift=0):
    pairs = []
    for z in range(Z):
        for x in range(X):
            for core in range(CORES):
                to = ((z + z_shift) % Z * X + (x + x_shift) % X) * CORES
                pairs.append(((z * X + x) * CORES + core, to + (core + core_shift) % CORES))
    return lax.ppermute(value, CTX, pairs)


def swap(value):
    return move(value, core_shift=1)


def exchange(sums):
    return lax.all_to_all(sums, ("core", "tp"), 0, 0, tiled=True)


def shape(dims, kind):
    return jax.ShapeDtypeStruct(dims, kind)


def shards(query_one, key_one, value_one, segments, query_base, key_two, value_two):
    segments_r = swap(segments)
    k1_r, v1_r, k2_r, v2_r = swap(key_one), swap(value_one), swap(key_two), swap(value_two)
    own0, state, query_send, info = call(
        prep_kernel,
        (
            shape((PAIR, 2 * HEAD_DIM), BF16),
            shape((144, HEAD_DIM), BF16),
            shape((2, TOK, COLS), BF16),
            shape((8,), jnp.int32),
        ),
        [ANY, SMEM] + [ANY, VMEM] * 4 + [ANY] * 2,
        (VMEM, VMEM, VMEM, SMEM),
        scratch=(
            pltpu.SMEM((TOK,), jnp.int32),
            pltpu.VMEM((TOK, HEAD_DIM), BF16),
            pltpu.VMEM((TOK, HEAD_DIM), BF16),
            pltpu.SemaphoreType.DMA((7,)),
        ),
        name="prep",
    )(
        segments, segments_r, key_one, k1_r, value_one, v1_r, key_two, k2_r, value_two, v2_r,
        query_one, query_base,
    )
    queries_r = swap(query_send)

    own1 = move(own0, z_shift=1)
    near = [move(state, x_shift=shift) for shift in (1, 2, 3)]
    prefix, plane = call(
        plane_kernel,
        (shape((HEAD_DIM + 8, HEAD_DIM), F32), shape((144, HEAD_DIM), BF16)),
        [SMEM] + [VMEM] * 4,
        (VMEM, VMEM),
        name="plane",
    )(info, state, *near)
    far = [move(plane, z_shift=back) for back in (1, 2, 3, 4)]

    own4 = move(own0, z_shift=4)
    own23 = move(jnp.concatenate([own0, own1], axis=0), z_shift=2)
    x = lax.axis_index("x")
    gathered = [move(own1, x_shift=shift) for shift in (1, 2, 3)]
    gathered += [
        move(jnp.where(x + shift < X, own0, own4), x_shift=shift) for shift in (1, 2, 3)
    ]
    gathered += [move(own23, x_shift=shift) for shift in (1, 2, 3)]

    inside, query = call(
        inside_kernel,
        (shape((PAIR, COLS), F32), shape((PAIR, COLS), BF16)),
        [SMEM] + [ANY, VMEM] * 3,
        (VMEM, VMEM),
        scratch=(
            pltpu.VMEM((PAIR, HEAD_DIM), BF16),
            pltpu.VMEM((PAIR, HEAD_DIM), BF16),
            pltpu.SemaphoreType.DMA((3,)),
        ),
        name="inside",
    )(info, query_one, queries_r, key_one, k1_r, value_one, v1_r)
    first, sums, reach = call(
        first_kernel,
        (
            shape((PAIR, COLS), F32),
            shape((CORES * TP, 8, PAIR), F32),
            shape((1,), jnp.int32),
        ),
        [SMEM] + [VMEM] * 7,
        (VMEM, VMEM, SMEM),
        name="first",
    )(info, prefix, *far, inside, query)

    mine, send, out_sums = call(
        attention_kernel,
        (
            shape((TOK, COLS), BF16),
            shape((TOK, COLS), BF16),
            shape((CORES * TP, 8, TOK), F32),
        ),
        [SMEM, SMEM, VMEM, VMEM, ANY, VMEM] + [ANY] * 13,
        (VMEM,) * 3,
        scratch=(
            pltpu.VMEM((PRIOR + PAIR, 3 * HEAD_DIM), BF16),
            pltpu.VMEM((REPEAT, PAIR, HEAD_DIM), BF16),
            pltpu.VMEM((REPEAT, PAIR, HEAD_DIM), F32),
            pltpu.VMEM((REPEAT, PAIR, 2 * HEAD_DIM), F32),
            pltpu.VMEM((PAIR, HEAD_DIM), F32),
            pltpu.VMEM((TOK, COLS), BF16),
            pltpu.SemaphoreType.DMA((21,)),
        ),
        limit=40 * 2**20,
        name="attention",
    )(info, reach, exchange(sums), first, query_base, queries_r, own0, own1, own23, own4, *gathered)
    theirs = swap(send)
    return call(
        last_kernel, shape((TOK, 2 * COLS), BF16), [VMEM] * 3, VMEM, name="last"
    )(exchange(out_sums), mine, theirs)


def solution(mesh):
    grid = Mesh(mesh.devices.reshape(Z, X, CORES, TP), ("z", "x", "core", "tp"))
    tokens, both = P(CTX), P(CTX, "tp")
    return jax.shard_map(
        shards,
        mesh=grid,
        in_specs=(both,) * 3 + (tokens,) + (both,) * 3,
        out_specs=both,
        check_vma=False,
    )
```

time: 124 us -> 132 us (1.065)
  the two profiles are of different devices: /device:TPU:128 before, /device:TPU:165 now
where the time goes in v2:
time: 132 us; the launch traced here: 133 us
  waiting for transfers between devices  45.5 us (34%)
  starting transfers between devices  43.8 us (33%)
  Pallas kernels  25.5 us (19%)
  local copies, waits for them, and re-layouts  9.97 us (8%)
  blocking collectives  7.71 us (6%)
    ppermute x26, waiting for transfers between devices, move(): return lax.ppermute(value, CTX, pairs)  40.5 us
    ppermute x26, starting transfers between devices, move(): return lax.ppermute(value, CTX, pairs)  24 us
    all_to_all x1, starting transfers between devices, exchange(): return lax.all_to_all(sums, ('core', 'tp'), 0, 0, tiled=True)  19.8 us
    pallas_call x1, Pallas kernels, shards(): call(attention_kernel, (shape((TOK, COLS), BF16), shape((TOK, COLS), BF16...  18.1 us
    unnamed x38, local copies, waits for them, and re-layouts  9.97 us
    all_to_all x1, blocking collectives, exchange(): return lax.all_to_all(sums, ('core', 'tp'), 0, 0, tiled=True)  7.71 us
    all_to_all x1, waiting for transfers between devices, exchange(): return lax.all_to_all(sums, ('core', 'tp'), 0, 0, tiled=True)  5 us
  transfers between devices with their start and end apart: 27, of which 9 were waited for; matrix products, arithmetic and copies ran while one was open for 0% of the time, Pallas kernels for 3%

profile of v2, /device:TPU:165, one launch (start us, length us, event | category | flops | bytes accessed | tf_op | source)
XLA Modules:
  0.0 132.7 jit_solution(9850660971603015616)
XLA Ops:
  1.7 1.0 collective-permute-done.seg_r
  9.0 1.9 %prep.1 = (bf16[384,256]{1,0:T(8,128)(2,1)S(1)}, bf16[144,128]{1,0:T(8,128)(2,1)S(1)}, bf16[2,192,512]{2,1,0:T(8,128)(2,1)S(1)}, s32[8]{0:T(128)S(1)}) custom-call(s32[192]{0:T(256)S(1)} %copy-done.18, s32[192]{0:T(256)S(1)} %collective-permute-done.seg_r, bf16[192,256]{1,0:T(8,128)(2,1)S(1)} %copy-done.4, bf16[192,256]{1,0:T(8,128)(2,1)S(1)} %collective-permute-done.1.k1_r, ...), custom_call_target="tpu_custom_call" | custom-call | tf_op jit(solution)/shard_map/prep/pallas_call | solution.py:423
  13.4 1.4 %collective-permute-start.12 = (bf16[2,192,512]{2,1,0:T(8,128)(2,1)S(1)}, bf16[2,192,512]{2,1,0:T(8,128)(2,1)S(1)}, u32[]{:S(2)}, u32[]{:S(2)}) collective-permute-start(bf16[2,192,512]{2,1,0:T(8,128)(2,1)S(1)} %get-tuple-element.23), channel_id=1, source_target_pairs={{0,4},{4,0},{8,12},{12,8},{16,20},{20,16},{24,28},{28,24},{32,36},... | collective-permute-start | bytes 1179656 | tf_op jit(solution)/shard_map/ppermute | solution.py:405
  14.9 2.3 %collective-permute-done.13.own1 = bf16[384,256]{1,0:T(8,128)(2,1)S(1)} collective-permute-done((bf16[384,256]{1,0:T(8,128)(2,1)S(1)}, bf16[384,256]{1,0:T(8,128)(2,1)S(1)}, u32[]{:S(2)}, u32[]{:S(2)}) %collective-permute-start.13) | collective-permute-done | bytes 196640 | tf_op jit(solution)/shard_map/ppermute | solution.py:405
  17.2 2.0 %collective-permute-start.14 = (bf16[768,256]{1,0:T(8,128)(2,1)S(1)}, bf16[768,256]{1,0:T(8,128)(2,1)S(1)}, u32[]{:S(2)}, u32[]{:S(2)}) collective-permute-start(bf16[768,256]{1,0:T(8,128)(2,1)S(1)} %pad_maximum_fusion), channel_id=1, source_target_pairs={{0,64},{4,68},{8,72},{12,76},{16,80},{20,84},{24,88},{28,92},{32,9... | collective-permute-start | bytes 1179656 | tf_op jit(solution)/shard_map/ppermute | solution.py:405
  19.2 2.5 %collective-permute-done.15.own4 = bf16[384,256]{1,0:T(8,128)(2,1)S(1)} collective-permute-done((bf16[384,256]{1,0:T(8,128)(2,1)S(1)}, bf16[384,256]{1,0:T(8,128)(2,1)S(1)}, u32[]{:S(2)}, u32[]{:S(2)}) %collective-permute-start.15) | collective-permute-done | bytes 196640 | tf_op jit(solution)/shard_map/ppermute | solution.py:405
  24.1 4.7 %collective-permute-done.7.from3 = bf16[144,128]{1,0:T(8,128)(2,1)S(1)} collective-permute-done((bf16[144,128]{1,0:T(8,128)(2,1)S(1)}, bf16[144,128]{1,0:T(8,128)(2,1)S(1)}, u32[]{:S(2)}, u32[]{:S(2)}) %collective-permute-start.7) | collective-permute-done | bytes 36896 | tf_op jit(solution)/shard_map/ppermute | solution.py:405
  29.4 5.6 %collective-permute-start.10 = (bf16[144,128]{1,0:T(8,128)(2,1)S(1)}, bf16[144,128]{1,0:T(8,128)(2,1)S(1)}, u32[]{:S(2)}, u32[]{:S(2)}) collective-permute-start(bf16[144,128]{1,0:T(8,128)(2,1)S(1)} %get-tuple-element.22), channel_id=1, source_target_pairs={{0,96},{4,100},{8,104},{12,108},{16,112},{20,116},{24,120},{28,124... | collective-permute-start | bytes 110600 | tf_op jit(solution)/shard_map/ppermute | solution.py:405
  35.0 15.5 %collective-permute-done.10.from3 = bf16[144,128]{1,0:T(8,128)(2,1)S(1)} collective-permute-done((bf16[144,128]{1,0:T(8,128)(2,1)S(1)}, bf16[144,128]{1,0:T(8,128)(2,1)S(1)}, u32[]{:S(2)}, u32[]{:S(2)}) %collective-permute-start.10) | collective-permute-done | bytes 36896 | tf_op jit(solution)/shard_map/ppermute | solution.py:405
  50.5 6.7 %collective-permute-done.11.from4 = bf16[144,128]{1,0:T(8,128)(2,1)S(1)} collective-permute-done((bf16[144,128]{1,0:T(8,128)(2,1)S(1)}, bf16[144,128]{1,0:T(8,128)(2,1)S(1)}, u32[]{:S(2)}, u32[]{:S(2)}) %collective-permute-start.11) | collective-permute-done | bytes 36896 | tf_op jit(solution)/shard_map/ppermute | solution.py:405
  57.3 2.8 %collective-permute-done.8.from1 = bf16[144,128]{1,0:T(8,128)(2,1)S(1)} collective-permute-done((bf16[144,128]{1,0:T(8,128)(2,1)S(1)}, bf16[144,128]{1,0:T(8,128)(2,1)S(1)}, u32[]{:S(2)}, u32[]{:S(2)}) %collective-permute-start.8) | collective-permute-done | bytes 36896 | tf_op jit(solution)/shard_map/ppermute | solution.py:405
  60.1 5.0 %collective-permute-done.9.from2 = bf16[144,128]{1,0:T(8,128)(2,1)S(1)} collective-permute-done((bf16[144,128]{1,0:T(8,128)(2,1)S(1)}, bf16[144,128]{1,0:T(8,128)(2,1)S(1)}, u32[]{:S(2)}, u32[]{:S(2)}) %collective-permute-start.9) | collective-permute-done | bytes 36896 | tf_op jit(solution)/shard_map/ppermute | solution.py:405
  65.4 1.1 collective-permute-start.16
  66.5 2.2 %collective-permute-start.22 = (bf16[768,256]{1,0:T(8,128)(2,1)S(1)}, bf16[768,256]{1,0:T(8,128)(2,1)S(1)}, u32[]{:S(2)}, u32[]{:S(2)}) collective-permute-start(bf16[768,256]{1,0:T(8,128)(2,1)S(1)} %collective-permute-done.14.own23), channel_id=1, source_target_pairs={{0,8},{4,12},{8,16},{12,20},{16,24},{20,28},{24,0},{28,4},{32,40},... | collective-permute-start | bytes 1179656 | tf_op jit(solution)/shard_map/ppermute | solution.py:405
  68.8 1.3 collective-permute-start.24
  70.0 1.8 %collective-permute-start.17 = (bf16[384,256]{1,0:T(8,128)(2,1)S(1)}, bf16[384,256]{1,0:T(8,128)(2,1)}, u32[]{:S(2)}, u32[]{:S(2)}) collective-permute-start(bf16[384,256]{1,0:T(8,128)(2,1)S(1)} %collective-permute-done.13.own1), channel_id=1, source_target_pairs={{0,16},{4,20},{8,24},{12,28},{16,0},{20,4},{24,8},{28,12},{32,48},... | collective-permute-start | bytes 589832 | tf_op jit(solution)/shard_map/ppermute | solution.py:405
  71.8 1.1 collective-permute-start.18
  73.0 2.0 %inside.1 = (f32[384,512]{1,0:T(8,128)S(1)}, bf16[384,512]{1,0:T(8,128)(2,1)S(1)}) custom-call(s32[8]{0:T(128)S(1)} %get-tuple-element.19.info, bf16[192,1024]{1,0:T(8,128)(2,1)S(1)} %copy-done.1, bf16[2,192,512]{2,1,0:T(8,128)(2,1)S(1)} %collective-permute-done.12.queries_r, bf16[192,256]{1,0:T(8,128)(2,1)S(1)} %copy-done.5, ...), custom_call_target="tpu_custom_call" | custom-call | tf_op jit(solution)/shard_map/inside/pallas_call | solution.py:466
  75.1 1.8 %first.1 = (f32[384,512]{1,0:T(8,128)S(1)}, f32[8,8,384]{2,1,0:T(8,128)}, s32[1]{0:T(128)}) custom-call(s32[8]{0:T(128)S(1)} %get-tuple-element.19.info, f32[136,128]{1,0:T(8,128)S(1)} %get-tuple-element.21.prefix, bf16[144,128]{1,0:T(8,128)(2,1)S(1)} %collective-permute-done.8.from1, bf16[144,128]{1,0:T(8,128)(2,1)S(1)} %collective-permute-done.9.from2, ...), custom_call_target="tpu_custom_call" | custom-call | tf_op jit(solution)/shard_map/first/pallas_call | solution.py:478
  76.9 19.8 %all-to-all-start = ((f32[8,8,384]{2,1,0:T(8,128)}), f32[8,8,384]{2,1,0:T(8,128)S(1)}, u32[]{:S(2)}, u32[]{:S(2)}) async-start(f32[8,8,384]{2,1,0:T(8,128)} %get-tuple-element.27), calls=%async_computation | async-start | bytes 196608 | tf_op jit(solution)/shard_map/all_to_all | solution.py:413
  96.7 5.0 %all-to-all-done.sums = f32[8,8,384]{2,1,0:T(8,128)S(1)} async-done(((f32[8,8,384]{2,1,0:T(8,128)}), f32[8,8,384]{2,1,0:T(8,128)S(1)}, u32[]{:S(2)}, u32[]{:S(2)}) %all-to-all-start) | async-done | bytes 98336 | tf_op jit(solution)/shard_map/all_to_all | solution.py:413
  105.4 18.1 %attention.1 = (bf16[192,512]{1,0:T(8,128)(2,1)S(1)}, bf16[192,512]{1,0:T(8,128)(2,1)S(1)}, f32[8,8,192]{2,1,0:T(8,128)S(1)}) custom-call(s32[8]{0:T(128)S(1)} %get-tuple-element.19.info, s32[1]{0:T(128)} %get-tuple-element.26.reach, f32[8,8,384]{2,1,0:T(8,128)S(1)} %all-to-all-done.sums, f32[384,512]{1,0:T(8,128)S(1)} %get-tuple-element.28.first, ...), custom_call_target="tpu_custom_call" | custom-call | tf_op jit(solution)/shard_map/attention/pallas_call | solution.py:490
  124.0 7.7 %all_to_all.10.sums = f32[8,8,192]{2,1,0:T(8,128)S(1)} all-to-all(f32[8,8,192]{2,1,0:T(8,128)S(1)} %get-tuple-element.30), channel_id=1, replica_groups=mesh['z'=8,'x'=4,'core'=2,'tp'=4] {'core','tp'}, dimensions={0} | all-to-all | bytes 98304 | tf_op jit(solution)/shard_map/all_to_all | solution.py:413
  131.7 1.0 last.1
  (77 shorter events, 18.2 us)
Async XLA Ops:
  0.0 2.7 %collective-permute-start.1 = (bf16[192,256]{1,0:T(8,128)(2,1)}, bf16[192,256]{1,0:T(8,128)(2,1)S(1)}, u32[]{:S(2)}, u32[]{:S(2)}) collective-permute-start(bf16[192,256]{1,0:T(8,128)(2,1)} %k1_any.3), channel_id=1, source_target_pairs={{0,4},{4,0},{8,12},{12,8},{16,20},{20,16},{24,28},{28,24},{32,36},... | collective-permute-start | bytes 294920 | tf_op jit(solution)/shard_map/ppermute | solution.py:405
  0.7 2.1 %collective-permute-start.2 = (bf16[192,256]{1,0:T(8,128)(2,1)}, bf16[192,256]{1,0:T(8,128)(2,1)S(1)}, u32[]{:S(2)}, u32[]{:S(2)}) collective-permute-start(bf16[192,256]{1,0:T(8,128)(2,1)} %v1_any.3), channel_id=1, source_target_pairs={{0,4},{4,0},{8,12},{12,8},{16,20},{20,16},{24,28},{28,24},{32,36},... | collective-permute-start | bytes 294920 | tf_op jit(solution)/shard_map/ppermute | solution.py:405
  10.9 6.2 %collective-permute-start.13 = (bf16[384,256]{1,0:T(8,128)(2,1)S(1)}, bf16[384,256]{1,0:T(8,128)(2,1)S(1)}, u32[]{:S(2)}, u32[]{:S(2)}) collective-permute-start(bf16[384,256]{1,0:T(8,128)(2,1)S(1)} %get-tuple-element.29.own0), channel_id=1, source_target_pairs={{0,32},{4,36},{8,40},{12,44},{16,48},{20,52},{24,56},{28,60},{32,6... | collective-permute-start | bytes 589832 | tf_op jit(solution)/shard_map/ppermute | solution.py:405
  11.7 9.9 %collective-permute-start.15 = (bf16[384,256]{1,0:T(8,128)(2,1)S(1)}, bf16[384,256]{1,0:T(8,128)(2,1)S(1)}, u32[]{:S(2)}, u32[]{:S(2)}) collective-permute-start(bf16[384,256]{1,0:T(8,128)(2,1)S(1)} %get-tuple-element.29.own0), channel_id=1, source_target_pairs={{0,128},{4,132},{8,136},{12,140},{16,144},{20,148},{24,152},{28,15... | collective-permute-start | bytes 589832 | tf_op jit(solution)/shard_map/ppermute | solution.py:405
  12.0 10.7 %collective-permute-start.5 = (bf16[144,128]{1,0:T(8,128)(2,1)S(1)}, bf16[144,128]{1,0:T(8,128)(2,1)S(1)}, u32[]{:S(2)}, u32[]{:S(2)}) collective-permute-start(bf16[144,128]{1,0:T(8,128)(2,1)S(1)} %get-tuple-element.20.own), channel_id=1, source_target_pairs={{0,8},{4,12},{8,16},{12,20},{16,24},{20,28},{24,0},{28,4},{32,40},... | collective-permute-start | bytes 110600 | tf_op jit(solution)/shard_map/ppermute | solution.py:405
  12.9 10.3 %collective-permute-start.6 = (bf16[144,128]{1,0:T(8,128)(2,1)S(1)}, bf16[144,128]{1,0:T(8,128)(2,1)S(1)}, u32[]{:S(2)}, u32[]{:S(2)}) collective-permute-start(bf16[144,128]{1,0:T(8,128)(2,1)S(1)} %get-tuple-element.20.own), channel_id=1, source_target_pairs={{0,16},{4,20},{8,24},{12,28},{16,0},{20,4},{24,8},{28,12},{32,48},... | collective-permute-start | bytes 110600 | tf_op jit(solution)/shard_map/ppermute | solution.py:405
  13.4 52.0 %collective-permute-start.12 = (bf16[2,192,512]{2,1,0:T(8,128)(2,1)S(1)}, bf16[2,192,512]{2,1,0:T(8,128)(2,1)S(1)}, u32[]{:S(2)}, u32[]{:S(2)}) collective-permute-start(bf16[2,192,512]{2,1,0:T(8,128)(2,1)S(1)} %get-tuple-element.23), channel_id=1, source_target_pairs={{0,4},{4,0},{8,12},{12,8},{16,20},{20,16},{24,28},{28,24},{32,36},... | collective-permute-start | bytes 1179656 | tf_op jit(solution)/shard_map/ppermute | solution.py:405
  17.2 49.3 %collective-permute-start.14 = (bf16[768,256]{1,0:T(8,128)(2,1)S(1)}, bf16[768,256]{1,0:T(8,128)(2,1)S(1)}, u32[]{:S(2)}, u32[]{:S(2)}) collective-permute-start(bf16[768,256]{1,0:T(8,128)(2,1)S(1)} %pad_maximum_fusion), channel_id=1, source_target_pairs={{0,64},{4,68},{8,72},{12,76},{16,80},{20,84},{24,88},{28,92},{32,9... | collective-permute-start | bytes 1179656 | tf_op jit(solution)/shard_map/ppermute | solution.py:405
  21.7 47.0 %collective-permute-start.19 = (bf16[384,256]{1,0:T(8,128)(2,1)S(1)}, bf16[384,256]{1,0:T(8,128)(2,1)S(1)}, u32[]{:S(2)}, u32[]{:S(2)}) collective-permute-start(bf16[384,256]{1,0:T(8,128)(2,1)S(1)} %get-tuple-element.35), channel_id=1, source_target_pairs={{0,8},{4,12},{8,16},{12,20},{16,24},{20,28},{24,0},{28,4},{32,40},... | collective-permute-start | bytes 589832 | tf_op jit(solution)/shard_map/ppermute | solution.py:405
  22.7 46.0 %collective-permute-start.20 = (bf16[384,256]{1,0:T(8,128)(2,1)S(1)}, bf16[384,256]{1,0:T(8,128)(2,1)S(1)}, u32[]{:S(2)}, u32[]{:S(2)}) collective-permute-start(bf16[384,256]{1,0:T(8,128)(2,1)S(1)} %get-tuple-element.34), channel_id=1, source_target_pairs={{0,16},{4,20},{8,24},{12,28},{16,0},{20,4},{24,8},{28,12},{32,48},... | collective-permute-start | bytes 589832 | tf_op jit(solution)/shard_map/ppermute | solution.py:405
  23.3 5.6 %collective-permute-start.7 = (bf16[144,128]{1,0:T(8,128)(2,1)S(1)}, bf16[144,128]{1,0:T(8,128)(2,1)S(1)}, u32[]{:S(2)}, u32[]{:S(2)}) collective-permute-start(bf16[144,128]{1,0:T(8,128)(2,1)S(1)} %get-tuple-element.20.own), channel_id=1, source_target_pairs={{0,24},{4,28},{8,0},{12,4},{16,8},{20,12},{24,16},{28,20},{32,56},... | collective-permute-start | bytes 110600 | tf_op jit(solution)/shard_map/ppermute | solution.py:405
  29.4 21.1 %collective-permute-start.10 = (bf16[144,128]{1,0:T(8,128)(2,1)S(1)}, bf16[144,128]{1,0:T(8,128)(2,1)S(1)}, u32[]{:S(2)}, u32[]{:S(2)}) collective-permute-start(bf16[144,128]{1,0:T(8,128)(2,1)S(1)} %get-tuple-element.22), channel_id=1, source_target_pairs={{0,96},{4,100},{8,104},{12,108},{16,112},{20,116},{24,120},{28,124... | collective-permute-start | bytes 110600 | tf_op jit(solution)/shard_map/ppermute | solution.py:405
  50.5 6.7 %collective-permute-start.11 = (bf16[144,128]{1,0:T(8,128)(2,1)S(1)}, bf16[144,128]{1,0:T(8,128)(2,1)S(1)}, u32[]{:S(2)}, u32[]{:S(2)}) collective-permute-start(bf16[144,128]{1,0:T(8,128)(2,1)S(1)} %get-tuple-element.22), channel_id=1, source_target_pairs={{0,128},{4,132},{8,136},{12,140},{16,144},{20,148},{24,152},{28,15... | collective-permute-start | bytes 110600 | tf_op jit(solution)/shard_map/ppermute | solution.py:405
  57.2 2.8 %collective-permute-start.8 = (bf16[144,128]{1,0:T(8,128)(2,1)S(1)}, bf16[144,128]{1,0:T(8,128)(2,1)S(1)}, u32[]{:S(2)}, u32[]{:S(2)}) collective-permute-start(bf16[144,128]{1,0:T(8,128)(2,1)S(1)} %get-tuple-element.22), channel_id=1, source_target_pairs={{0,32},{4,36},{8,40},{12,44},{16,48},{20,52},{24,56},{28,60},{32,6... | collective-permute-start | bytes 110600 | tf_op jit(solution)/shard_map/ppermute | solution.py:405
  60.1 5.0 %collective-permute-start.9 = (bf16[144,128]{1,0:T(8,128)(2,1)S(1)}, bf16[144,128]{1,0:T(8,128)(2,1)S(1)}, u32[]{:S(2)}, u32[]{:S(2)}) collective-permute-start(bf16[144,128]{1,0:T(8,128)(2,1)S(1)} %get-tuple-element.22), channel_id=1, source_target_pairs={{0,64},{4,68},{8,72},{12,76},{16,80},{20,84},{24,88},{28,92},{32,9... | collective-permute-start | bytes 110600 | tf_op jit(solution)/shard_map/ppermute | solution.py:405
  65.0 5.0 %collective-permute-start.21 = (bf16[384,256]{1,0:T(8,128)(2,1)S(1)}, bf16[384,256]{1,0:T(8,128)(2,1)S(1)}, u32[]{:S(2)}, u32[]{:S(2)}) collective-permute-start(bf16[384,256]{1,0:T(8,128)(2,1)S(1)} %get-tuple-element.33), channel_id=1, source_target_pairs={{0,24},{4,28},{8,0},{12,4},{16,8},{20,12},{24,16},{28,20},{32,56},... | collective-permute-start | bytes 589832 | tf_op jit(solution)/shard_map/ppermute | solution.py:405
  65.4 6.4 %collective-permute-start.16 = (bf16[384,256]{1,0:T(8,128)(2,1)S(1)}, bf16[384,256]{1,0:T(8,128)(2,1)S(1)}, u32[]{:S(2)}, u32[]{:S(2)}) collective-permute-start(bf16[384,256]{1,0:T(8,128)(2,1)S(1)} %collective-permute-done.13.own1), channel_id=1, source_target_pairs={{0,8},{4,12},{8,16},{12,20},{16,24},{20,28},{24,0},{28,4},{32,40},... | collective-permute-start | bytes 589832 | tf_op jit(solution)/shard_map/ppermute | solution.py:405
  66.5 35.2 %collective-permute-start.22 = (bf16[768,256]{1,0:T(8,128)(2,1)S(1)}, bf16[768,256]{1,0:T(8,128)(2,1)S(1)}, u32[]{:S(2)}, u32[]{:S(2)}) collective-permute-start(bf16[768,256]{1,0:T(8,128)(2,1)S(1)} %collective-permute-done.14.own23), channel_id=1, source_target_pairs={{0,8},{4,12},{8,16},{12,20},{16,24},{20,28},{24,0},{28,4},{32,40},... | collective-permute-start | bytes 1179656 | tf_op jit(solution)/shard_map/ppermute | solution.py:405
  68.8 32.9 %collective-permute-start.23 = (bf16[768,256]{1,0:T(8,128)(2,1)S(1)}, bf16[768,256]{1,0:T(8,128)(2,1)S(1)}, u32[]{:S(2)}, u32[]{:S(2)}) collective-permute-start(bf16[768,256]{1,0:T(8,128)(2,1)S(1)} %collective-permute-done.14.own23), channel_id=1, source_target_pairs={{0,16},{4,20},{8,24},{12,28},{16,0},{20,4},{24,8},{28,12},{32,48},... | collective-permute-start | bytes 1179656 | tf_op jit(solution)/shard_map/ppermute | solution.py:405
  68.8 32.9 %collective-permute-start.24 = (bf16[768,256]{1,0:T(8,128)(2,1)S(1)}, bf16[768,256]{1,0:T(8,128)(2,1)}, u32[]{:S(2)}, u32[]{:S(2)}) collective-permute-start(bf16[768,256]{1,0:T(8,128)(2,1)S(1)} %collective-permute-done.14.own23), channel_id=1, source_target_pairs={{0,24},{4,28},{8,0},{12,4},{16,8},{20,12},{24,16},{28,20},{32,56},... | collective-permute-start | bytes 1179656 | tf_op jit(solution)/shard_map/ppermute | solution.py:405
  70.0 26.6 %collective-permute-start.17 = (bf16[384,256]{1,0:T(8,128)(2,1)S(1)}, bf16[384,256]{1,0:T(8,128)(2,1)}, u32[]{:S(2)}, u32[]{:S(2)}) collective-permute-start(bf16[384,256]{1,0:T(8,128)(2,1)S(1)} %collective-permute-done.13.own1), channel_id=1, source_target_pairs={{0,16},{4,20},{8,24},{12,28},{16,0},{20,4},{24,8},{28,12},{32,48},... | collective-permute-start | bytes 589832 | tf_op jit(solution)/shard_map/ppermute | solution.py:405
  71.8 24.8 %collective-permute-start.18 = (bf16[384,256]{1,0:T(8,128)(2,1)S(1)}, bf16[384,256]{1,0:T(8,128)(2,1)}, u32[]{:S(2)}, u32[]{:S(2)}) collective-permute-start(bf16[384,256]{1,0:T(8,128)(2,1)S(1)} %collective-permute-done.13.own1), channel_id=1, source_target_pairs={{0,24},{4,28},{8,0},{12,4},{16,8},{20,12},{24,16},{28,20},{32,56},... | collective-permute-start | bytes 589832 | tf_op jit(solution)/shard_map/ppermute | solution.py:405
  76.9 24.8 %all-to-all-start = ((f32[8,8,384]{2,1,0:T(8,128)}), f32[8,8,384]{2,1,0:T(8,128)S(1)}, u32[]{:S(2)}, u32[]{:S(2)}) async-start(f32[8,8,384]{2,1,0:T(8,128)} %get-tuple-element.27), calls=%async_computation | async-start | bytes 196608 | tf_op jit(solution)/shard_map/all_to_all | solution.py:413
  123.5 8.2 %collective-permute-start.25 = (bf16[192,512]{1,0:T(8,128)(2,1)S(1)}, bf16[192,512]{1,0:T(8,128)(2,1)S(1)}, u32[]{:S(2)}, u32[]{:S(2)}) collective-permute-start(bf16[192,512]{1,0:T(8,128)(2,1)S(1)} %get-tuple-element.32), channel_id=1, source_target_pairs={{0,4},{4,0},{8,12},{12,8},{16,20},{20,16},{24,28},{28,24},{32,36},... | collective-permute-start | bytes 589832 | tf_op jit(solution)/shard_map/ppermute | solution.py:405
  (22 other events, 220.9 us)

commit v3 on v2

v3 whole, which is shorter than its diff:
```python
import jax
import jax.numpy as jnp
from jax import lax
from jax.experimental import pallas as pl
from jax.experimental.pallas import tpu as pltpu
from jax.sharding import Mesh, PartitionSpec as P

HEAD_DIM = 128
WIDTH = 4096
EPSILON = 1e-05
NEGATIVE = -1e30

TOK = 192
PAIR = 384
REPEAT = 4
COLS = REPEAT * HEAD_DIM
Z, X, CORES, TP = 8, 4, 2, 4
CHUNK = 2
SCALE = HEAD_DIM ** (-0.5) * 1.4426950408889634

F32 = jnp.float32
BF16 = jnp.bfloat16
VMEM = pl.BlockSpec(memory_space=pltpu.VMEM)
SMEM = pl.BlockSpec(memory_space=pltpu.SMEM)
HBM = pl.BlockSpec(memory_space=pltpu.HBM)


def place():
    return lax.axis_index("z"), lax.axis_index("x"), lax.axis_index("core")


def call(kernel, outs, specs_in, specs_out, scratch=(), aliases=None, limit=16, name=None):
    return pl.pallas_call(
        kernel,
        out_shape=outs,
        in_specs=specs_in,
        out_specs=specs_out,
        scratch_shapes=list(scratch),
        input_output_aliases=aliases or {},
        compiler_params=pltpu.CompilerParams(vmem_limit_bytes=limit * 2**20),
        name=name,
    )


def count_below(ref, doc):
    found = jnp.int32(0)
    for step in (128, 64, 32, 16, 8, 4, 2, 1):
        tried = found + step
        last = ref[jnp.minimum(tried, TOK) - 1]
        found = jnp.where((tried <= TOK) & (last < doc), tried, found)
    return found


def half(core):
    return pl.ds(pl.multiple_of(core * HEAD_DIM, HEAD_DIM), HEAD_DIM)


def rows_of(core):
    return pl.ds(pl.multiple_of(core * TOK, 64), TOK)


def prep_kernel(seg, seg_r, own, other, own0_ref, first_ref, state_ref, info_ref):
    core = place()[2]
    for side, ref in ((core, own), (1 - core, other)):
        first_ref[rows_of(side), :HEAD_DIM] = ref[0]
        first_ref[rows_of(side), HEAD_DIM:] = ref[1]
        own0_ref[rows_of(side), :HEAD_DIM] = ref[2]
        own0_ref[rows_of(side), HEAD_DIM:] = ref[3]
    below = [count_below(seg, d) for d in (1, 2, 3)]
    below_r = [count_below(seg_r, d) for d in (1, 2, 3)]
    bounds = [a + b for a, b in zip(below, below_r)]
    first = jnp.where(core == 0, seg[0], seg_r[0])
    last = jnp.where(core == 0, seg_r[TOK - 1], seg[TOK - 1])

    def pick(values, doc):
        out = jnp.int32(0)
        for d in (1, 2, 3):
            out = jnp.where(doc == d, values[d - 1], out)
        return out

    count = PAIR - pick(bounds, last)
    first_end = jnp.where(first == 3, PAIR, pick(bounds, first + 1))
    for place_in, value in enumerate((*bounds, first, last, count, first_end, 0)):
        info_ref[place_in] = jnp.int32(value)
    rows = lax.broadcasted_iota(jnp.int32, (PAIR, HEAD_DIM), 0)
    masked = jnp.where(rows >= PAIR - count, first_ref[:, :HEAD_DIM].astype(F32), 0.0)
    state = lax.dot_general(
        masked.astype(BF16),
        first_ref[:, HEAD_DIM:],
        (((0,), (0,)), ((), ())),
        preferred_element_type=F32,
    )
    state_ref[:HEAD_DIM] = state.astype(BF16)
    state_ref[HEAD_DIM:] = notes(last.astype(F32), count.astype(F32)).astype(BF16)


def notes(last, count):
    row = lax.broadcasted_iota(jnp.int32, (16, HEAD_DIM), 0)
    high = jnp.floor(count * (1.0 / 64.0))
    return jnp.where(
        row == 0, last, jnp.where(row == 1, high, jnp.where(row == 2, count - 64.0 * high, 0.0))
    )


def read_state(ref):
    tail = ref[HEAD_DIM:].astype(F32)
    return ref[:HEAD_DIM].astype(F32), tail[0:1], tail[1:2] * 64.0 + tail[2:3]


def plane_kernel(
    info, own, from1, from2, from3, own0, own1, queries_r, prefix_ref, plane_ref, own01_ref
):
    x = place()[1]
    own01_ref[:PAIR] = own0[...]
    own01_ref[PAIR:] = own1[...]
    first = info[3].astype(F32)
    items = [read_state(ref) for ref in (own, from1, from2, from3)]
    prefix = jnp.zeros((HEAD_DIM, HEAD_DIM), F32)
    prefix_count = jnp.zeros((1, HEAD_DIM), F32)
    for shift in (1, 2, 3):
        state, doc, count = items[shift]
        chosen = jnp.where((doc == first) & (x >= shift), 1.0, 0.0)
        prefix += state * chosen
        prefix_count += count * chosen
    prefix_ref[:HEAD_DIM] = prefix
    prefix_ref[HEAD_DIM:] = jnp.broadcast_to(prefix_count, (8, HEAD_DIM))
    last = items[0][1]
    for item in items[1:]:
        last = jnp.maximum(last, item[1])
    total = jnp.zeros((HEAD_DIM, HEAD_DIM), F32)
    total_count = jnp.zeros((1, HEAD_DIM), F32)
    for state, doc, count in items:
        chosen = jnp.where(doc == last, 1.0, 0.0)
        total += state * chosen
        total_count += count * chosen
    plane_ref[:HEAD_DIM] = total.astype(BF16)
    plane_ref[HEAD_DIM:] = notes(last, total_count).astype(BF16)


def document_start(info, rows):
    start = jnp.zeros_like(rows)
    for d in range(3):
        start = jnp.where(rows >= info[d], jnp.maximum(start, info[d]), start)
    return start


def split_dot(wide, narrow):
    high = wide.astype(BF16)
    low = (wide - high.astype(F32)).astype(BF16)
    return jnp.dot(high, narrow, preferred_element_type=F32) + jnp.dot(
        low, narrow, preferred_element_type=F32
    )


def inside_kernel(info, keep, queries_r, packed, inside_ref, query_ref):
    core = place()[2]
    query_ref[rows_of(core), :] = keep[0]
    query_ref[rows_of(1 - core), :] = queries_r[0]
    row = lax.broadcasted_iota(jnp.int32, (PAIR, PAIR), 0)
    column = lax.broadcasted_iota(jnp.int32, (PAIR, PAIR), 1)
    visible = (column <= row) & (column >= document_start(info, row))
    for head in range(REPEAT):
        cols = slice(head * HEAD_DIM, (head + 1) * HEAD_DIM)
        scores = lax.dot_general(
            query_ref[:, cols],
            packed[:, :HEAD_DIM],
            (((1,), (1,)), ((), ())),
            preferred_element_type=F32,
        )
        scores = jnp.where(visible, scores, 0.0)
        inside_ref[:, cols] = split_dot(scores, packed[:, HEAD_DIM:])


def row_sums(squares):
    high = squares.astype(BF16)
    low = (squares - high.astype(F32)).astype(BF16)
    ones = jnp.ones((8, squares.shape[1]), BF16)
    dims = (((1,), (1,)), ((), ()))
    return lax.dot_general(ones, high, dims, preferred_element_type=F32) + lax.dot_general(
        ones, low, dims, preferred_element_type=F32
    )


def first_kernel(
    info, prefix, from1, from2, from3, from4, inside, query, first_ref, sums_ref, count_ref
):
    z = place()[0]
    first = info[3].astype(F32)
    state = prefix[:HEAD_DIM]
    count = prefix[HEAD_DIM : HEAD_DIM + 1]
    for back, ref in enumerate((from1, from2, from3, from4), 1):
        one_state, doc, one_count = read_state(ref)
        chosen = jnp.where((doc == first) & (z >= back), 1.0, 0.0)
        state += one_state * chosen
        count += one_count * chosen
    count_ref[0] = jnp.max(count).astype(jnp.int32)
    high = state.astype(BF16)
    low = (state - high.astype(F32)).astype(BF16)
    in_first = lax.broadcasted_iota(jnp.int32, (PAIR, HEAD_DIM), 0) < info[6]
    squares = jnp.zeros((PAIR, HEAD_DIM), F32)
    for head in range(REPEAT):
        cols = slice(head * HEAD_DIM, (head + 1) * HEAD_DIM)
        queries = query[:, cols]
        earlier = jnp.dot(queries, high, preferred_element_type=F32) + jnp.dot(
            queries, low, preferred_element_type=F32
        )
        out = inside[:, cols] + jnp.where(in_first, earlier, 0.0)
        first_ref[:, cols] = out
        squares += out * out
    sums = row_sums(squares)
    for to in range(CORES * TP):
        sums_ref[to] = sums


def row_scale(sums):
    total = sums[0]
    for device in range(1, CORES * TP):
        total = total + sums[device]
    return lax.transpose(lax.rsqrt(total * (1.0 / WIDTH) + EPSILON), (1, 0))[:, :1]


TILE = 128
TILES = [(head, slice(at, at + TILE)) for head in range(REPEAT) for at in range(0, PAIR, TILE)]


def scores_of(queries, keys, head, part, rows):
    return lax.dot_general(
        queries[head, part],
        keys[rows, :HEAD_DIM],
        (((1,), (1,)), ((), ())),
        preferred_element_type=F32,
    )


def sweep(queries, kv, tops, acc, rows, visible=None, begin=False):
    ahead = scores_of(queries, kv, *TILES[0], rows)
    for at, (head, part) in enumerate(TILES):
        scores = ahead
        if at + 1 < len(TILES):
            ahead = scores_of(queries, kv, *TILES[at + 1], rows)
        if visible is not None:
            scores = jnp.where(visible(part), scores, NEGATIVE)
        top = jnp.max(scores, axis=1, keepdims=True)
        if begin:
            top = jnp.broadcast_to(top, (TILE, HEAD_DIM))
        else:
            old_top = tops[head, part]
            top = jnp.maximum(old_top, top)
        wide_top = jnp.concatenate([top] * (scores.shape[1] // HEAD_DIM), axis=1)
        weights = jnp.exp2((scores - wide_top) * SCALE)
        summed = jnp.dot(weights.astype(BF16), kv[rows, HEAD_DIM:], preferred_element_type=F32)
        tops[head, part] = top
        if begin:
            acc[head, part] = summed
        else:
            shrink = jnp.exp2((old_top - top) * SCALE)
            acc[head, part] = acc[head, part] * jnp.concatenate([shrink, shrink], axis=1) + summed


class Window:
    def __init__(self, info, prior, blocks, kv, bounds, sems):
        self.info, self.kv, self.bounds = info, kv, bounds
        used = jnp.int32(0)
        self.copies = []
        for at, (ref, distance) in enumerate(blocks):
            distance = jnp.int32(distance)
            needed = (distance >= 1) & (distance <= 16) & (prior > (distance - 1) * PAIR)
            slot = jnp.minimum(used, bounds.shape[0] - 1)
            rows = pl.ds(pl.multiple_of(slot * PAIR, PAIR), PAIR)
            copy = pltpu.make_async_copy(ref, kv.at[rows, pl.ds(0, 2 * HEAD_DIM)], sems.at[at])
            self.copies.append((needed, copy))

            @pl.when(needed)
            def _():
                copy.start()
                bounds[slot] = jnp.maximum(distance * PAIR - prior, 0)

            used = used + needed.astype(jnp.int32)
        self.steps = (used + CHUNK - 1) // CHUNK
        kv[:, 2 * HEAD_DIM :] = jnp.ones((kv.shape[0], HEAD_DIM), BF16)

        @pl.when(used % CHUNK != 0)
        def _():
            rows = pl.ds(pl.multiple_of(used * PAIR, PAIR), PAIR)
            kv[rows, : 2 * HEAD_DIM] = jnp.zeros((PAIR, 2 * HEAD_DIM), BF16)
            bounds[used] = jnp.int32(PAIR)

    def absorb(self, queries, tops, acc):
        for needed, copy in self.copies:
            pl.when(needed)(copy.wait)

        @pl.loop(0, self.steps)
        def _(step):
            rows = pl.ds(pl.multiple_of(step * CHUNK * PAIR, CHUNK * PAIR), CHUNK * PAIR)
            low0, low1 = self.bounds[step * CHUNK], self.bounds[step * CHUNK + 1]
            first_end = self.info[6]
            whole = (low0 == 0) & (low1 == 0) & (first_end == PAIR)

            @pl.when(whole)
            def _():
                sweep(queries, self.kv, tops, acc, rows)

            @pl.when(jnp.logical_not(whole))
            def _():
                def visible(part):
                    row = lax.broadcasted_iota(jnp.int32, (TILE, CHUNK * PAIR), 0) + part.start
                    column = lax.broadcasted_iota(jnp.int32, (TILE, CHUNK * PAIR), 1)
                    low = jnp.where(column < PAIR, low0, PAIR + low1)
                    return (column >= low) & (row < first_end)

                sweep(queries, self.kv, tops, acc, rows, visible)


SLOTS = 10


def near_kernel(
    info, reach, sums, first, keep, queries_r, own0, near_hbm, own23,
    queries, tops, acc, kv, own, scales, bounds, sems
):
    _, x, core = place()
    blocks = []
    for other in range(X):
        at = 2 * PAIR * other
        blocks.append((near_hbm.at[pl.ds(at + PAIR, PAIR)], 4 + x - other))
        if other < X - 1:
            blocks.append((near_hbm.at[pl.ds(at, PAIR)], x - other))
    blocks += [(own23.at[pl.ds(0, PAIR)], 8), (own23.at[pl.ds(PAIR, PAIR)], 12)]
    window = Window(info, reach[0], blocks, kv, bounds, sems)
    own[:, : 2 * HEAD_DIM] = own0[...]
    own[:, 2 * HEAD_DIM :] = jnp.ones((PAIR, HEAD_DIM), BF16)
    scales[...] = jnp.broadcast_to(row_scale(sums), (PAIR, HEAD_DIM))
    for part, where in ((keep.at[1], rows_of(core)), (queries_r.at[1], rows_of(1 - core))):
        for head in range(REPEAT):
            cols = slice(head * HEAD_DIM, (head + 1) * HEAD_DIM)
            value = part[:, cols].astype(F32) + first[where, cols] * scales[where, :]
            queries[head, where, :] = value.astype(BF16)

    def own_visible(part):
        row = lax.broadcasted_iota(jnp.int32, (TILE, PAIR), 0) + part.start
        column = lax.broadcasted_iota(jnp.int32, (TILE, PAIR), 1)
        return (column <= row) & (column >= document_start(info, row))

    sweep(queries, own, tops, acc, slice(0, PAIR), own_visible, begin=True)
    window.absorb(queries, tops, acc)


def far_kernel(
    info, reach, queries, old_tops, old_acc, own4, last1, last2, last3, far1, far2, far3,
    mine_ref, send_ref, sums_ref, tops, acc, kv, bounds, sems
):
    _, x, core = place()
    blocks = [(own4, 16)]
    for shift, last, far in zip((1, 2, 3), (last1, last2, last3), (far1, far2, far3)):
        wrapped = jnp.where(x < shift, 4, 0)
        blocks.append((far.at[pl.ds(0, PAIR)], 8 + shift - wrapped))
        blocks.append((far.at[pl.ds(PAIR, PAIR)], 12 + shift - wrapped))
        blocks.append((last, jnp.where(x < shift, 12 + shift, 0)))
    window = Window(info, reach[0], blocks, kv, bounds, sems)
    window.absorb(queries, tops, acc)
    for side in range(CORES):
        where = slice(side * TOK, (side + 1) * TOK)
        squares = jnp.zeros((TOK, HEAD_DIM), F32)
        outs = []
        for head in range(REPEAT):
            summed = acc[head, where, :]
            out = (summed[:, :HEAD_DIM] / summed[:, HEAD_DIM:]).astype(BF16)
            outs.append(out)
            widened = out.astype(F32)
            squares += widened * widened
        whole = jnp.concatenate(outs, axis=1)

        @pl.when(core == side)
        def _():
            mine_ref[...] = whole

        @pl.when(core != side)
        def _():
            send_ref[...] = whole

        sums = row_sums(squares)
        for to in range(TP):
            sums_ref[side * TP + to] = sums


def last_kernel(sums, mine, theirs, out_ref):
    core = place()[2]
    scale = row_scale(sums)
    for ref, side in ((mine, core), (theirs, 1 - core)):
        cols = pl.ds(pl.multiple_of(side * COLS, COLS), COLS)
        out_ref[:, cols] = (ref[...].astype(F32) * scale).astype(BF16)


CTX = ("z", "x", "core")


def move(value, z_shift=0, x_shift=0, core_shift=0, keep=lambda x: True):
    pairs = []
    for z in range(Z):
        for x in range(X):
            for core in range(CORES):
                to = ((z + z_shift) % Z * X + (x + x_shift) % X) * CORES
                if keep(x):
                    pairs.append(((z * X + x) * CORES + core, to + (core + core_shift) % CORES))
    return lax.ppermute(value, CTX, pairs)


def swap(value):
    return move(value, core_shift=1)


def exchange(sums):
    return lax.all_to_all(sums, ("core", "tp"), 0, 0, tiled=True)


def shape(dims, kind):
    return jax.ShapeDtypeStruct(dims, kind)


def shards(query_one, key_one, value_one, segments, query_base, key_two, value_two):
    core = lax.axis_index("core")

    def halves(arrays):
        low = jnp.stack([array[:, : array.shape[1] // 2] for array in arrays])
        high = jnp.stack([array[:, array.shape[1] // 2 :] for array in arrays])
        return jnp.where(core == 0, low, high), jnp.where(core == 0, high, low)

    segments_r = swap(segments)
    own_keep, own_send = halves((key_one, value_one, key_two, value_two))
    own0, packed, state, info = call(
        prep_kernel,
        (
            shape((PAIR, 2 * HEAD_DIM), BF16),
            shape((PAIR, 2 * HEAD_DIM), BF16),
            shape((144, HEAD_DIM), BF16),
            shape((8,), jnp.int32),
        ),
        [SMEM, SMEM, VMEM, VMEM],
        (VMEM,) * 3 + (SMEM,),
        name="prep",
    )(segments, segments_r, own_keep, swap(own_send))
    keep, query_send = halves((query_one, query_base))
    queries_r = swap(query_send)

    own1 = move(own0, z_shift=1)
    near = [move(state, x_shift=shift) for shift in (1, 2, 3)]
    prefix, plane, own01 = call(
        plane_kernel,
        (
            shape((HEAD_DIM + 8, HEAD_DIM), F32),
            shape((144, HEAD_DIM), BF16),
            shape((2 * PAIR, 2 * HEAD_DIM), BF16),
        ),
        [SMEM] + [VMEM] * 7,
        (VMEM,) * 3,
        name="plane",
    )(info, state, *near, own0, own1, queries_r)
    far = [move(plane, z_shift=back) for back in (1, 2, 3, 4)]
    own23 = move(own01, z_shift=2)
    near_packs = lax.all_gather(own01, "x", axis=0, tiled=True)

    inside, query = call(
        inside_kernel,
        (shape((PAIR, COLS), F32), shape((PAIR, COLS), BF16)),
        [SMEM] + [VMEM] * 3,
        (VMEM,) * 2,
        name="inside",
    )(info, keep, queries_r, packed)
    first, sums, reach = call(
        first_kernel,
        (
            shape((PAIR, COLS), F32),
            shape((CORES * TP, 8, PAIR), F32),
            shape((1,), jnp.int32),
        ),
        [SMEM] + [VMEM] * 7,
        (VMEM, VMEM, SMEM),
        name="first",
    )(info, prefix, *far, inside, query)


    def once_known(value):
        return jnp.where(reach[0] >= 0, value, jnp.zeros_like(value))

    own4 = move(once_known(own0), z_shift=4)
    later23 = once_known(own23)
    far23 = [move(later23, x_shift=shift) for shift in (1, 2, 3)]
    far4 = [move(own4, x_shift=shift, keep=lambda x: x + shift >= X) for shift in (1, 2, 3)]
    queries, tops, acc = call(
        near_kernel,
        (
            shape((REPEAT, PAIR, HEAD_DIM), BF16),
            shape((REPEAT, PAIR, HEAD_DIM), F32),
            shape((REPEAT, PAIR, 2 * HEAD_DIM), F32),
        ),
        [SMEM, SMEM] + [VMEM] * 5 + [HBM, VMEM],
        (VMEM,) * 3,
        scratch=(
            pltpu.VMEM((SLOTS * PAIR, 3 * HEAD_DIM), BF16),
            pltpu.VMEM((PAIR, 3 * HEAD_DIM), BF16),
            pltpu.VMEM((PAIR, HEAD_DIM), F32),
            pltpu.SMEM((SLOTS,), jnp.int32),
            pltpu.SemaphoreType.DMA((9,)),
        ),
        name="near",
    )(info, reach, exchange(sums), first, keep, queries_r, own0, near_packs, own23)
    mine, send, out_sums, _, _ = call(
        far_kernel,
        (
            shape((TOK, COLS), BF16),
            shape((TOK, COLS), BF16),
            shape((CORES * TP, 8, TOK), F32),
            shape((REPEAT, PAIR, HEAD_DIM), F32),
            shape((REPEAT, PAIR, 2 * HEAD_DIM), F32),
        ),
        [SMEM, SMEM] + [VMEM] * 10,
        (VMEM,) * 5,
        scratch=(
            pltpu.VMEM((SLOTS * PAIR, 3 * HEAD_DIM), BF16),
            pltpu.SMEM((SLOTS,), jnp.int32),
            pltpu.SemaphoreType.DMA((10,)),
        ),
        aliases={3: 3, 4: 4},
        name="far",
    )(info, reach, queries, tops, acc, own4, *far4, *far23)
    theirs = swap(send)
    return call(
        last_kernel, shape((TOK, 2 * COLS), BF16), [VMEM] * 3, VMEM, name="last"
    )(exchange(out_sums), mine, theirs)


def solution(mesh):
    grid = Mesh(mesh.devices.reshape(Z, X, CORES, TP), ("z", "x", "core", "tp"))
    tokens, both = P(CTX), P(CTX, "tp")
    return jax.shard_map(
        shards,
        mesh=grid,
        in_specs=(both,) * 3 + (tokens,) + (both,) * 3,
        out_specs=both,
        check_vma=False,
    )
```

time: 132 us -> 123 us (0.932)
  the two profiles are of different devices: /device:TPU:165 before, /device:TPU:71 now
where the time goes in v3:
time: 123 us; the launch traced here: 124 us
  starting transfers between devices  32.8 us (27%)
  waiting for transfers between devices  26.2 us (21%)
  Pallas kernels  25.7 us (21%)
  blocking collectives  19.8 us (16%)
  between operations  14.1 us (11%)
  local copies, waits for them, and re-layouts  4.01 us (3%)
    ppermute x20, starting transfers between devices, move(): return lax.ppermute(value, CTX, pairs)  32.8 us
    ppermute x20, waiting for transfers between devices, move(): return lax.ppermute(value, CTX, pairs)  26.2 us
    all_to_all x2, blocking collectives, exchange(): return lax.all_to_all(sums, ('core', 'tp'), 0, 0, tiled=True)  19.8 us
    pallas_call x1, Pallas kernels, shards(): call(near_kernel, (shape((REPEAT, PAIR, HEAD_DIM), BF16), shape((REPEAT,...  11.5 us
    pallas_call x1, Pallas kernels, shards(): call(far_kernel, (shape((TOK, COLS), BF16), shape((TOK, COLS), BF16), sha...  7 us
  transfers between devices with their start and end apart: 21, of which 6 were waited for; matrix products, arithmetic and copies ran while one was open for 1% of the time, Pallas kernels for 13%

profile of v3, /device:TPU:71, one launch (start us, length us, event | category | flops | bytes accessed | tf_op | source)
XLA Modules:
  0.0 123.5 jit_solution(17736439456805829468)
XLA Ops:
  6.5 1.0 slice_bitcast_fusion.10
  10.0 1.2 collective-permute-done.seg_r
  11.2 1.4 %prep.1 = (bf16[384,256]{1,0:T(8,128)(2,1)S(1)}, bf16[384,256]{1,0:T(8,128)(2,1)S(1)}, bf16[144,128]{1,0:T(8,128)(2,1)S(1)}, s32[8]{0:T(128)S(1)}) custom-call(s32[192]{0:T(256)S(1)} %copy-done.3, s32[192]{0:T(256)S(1)} %collective-permute-done.seg_r, bf16[4,192,128]{2,1,0:T(8,128)(2,1)S(1)} %get-tuple-element.48.own, ...), custom_call_target="tpu_custom_call" | custom-call | tf_op jit(solution)/shard_map/prep/pallas_call | solution.py:430
  12.6 1.7 %collective-permute-start.5 = (bf16[384,256]{1,0:T(8,128)(2,1)S(1)}, bf16[384,256]{1,0:T(8,128)(2,1)S(1)}, u32[]{:S(2)}, u32[]{:S(2)}) collective-permute-start(bf16[384,256]{1,0:T(8,128)(2,1)S(1)} %get-tuple-element.25.own0), channel_id=1, source_target_pairs={{0,32},{4,36},{8,40},{12,44},{16,48},{20,52},{24,56},{28,60},{32,6... | collective-permute-start | bytes 589832 | tf_op jit(solution)/shard_map/ppermute | solution.py:405
  15.7 1.8 %collective-permute-start.2 = (bf16[144,128]{1,0:T(8,128)(2,1)S(1)}, bf16[144,128]{1,0:T(8,128)(2,1)S(1)}, u32[]{:S(2)}, u32[]{:S(2)}) collective-permute-start(bf16[144,128]{1,0:T(8,128)(2,1)S(1)} %get-tuple-element.24.own), channel_id=1, source_target_pairs={{0,8},{4,12},{8,16},{12,20},{16,24},{20,28},{24,0},{28,4},{32,40},... | collective-permute-start | bytes 110600 | tf_op jit(solution)/shard_map/ppermute | solution.py:405
  19.6 1.3 %plane.1 = (f32[136,128]{1,0:T(8,128)S(1)}, bf16[144,128]{1,0:T(8,128)(2,1)S(1)}, bf16[768,256]{1,0:T(8,128)(2,1)}) custom-call(s32[8]{0:T(128)S(1)} %get-tuple-element.23.info, bf16[144,128]{1,0:T(8,128)(2,1)S(1)} %get-tuple-element.24.own, bf16[144,128]{1,0:T(8,128)(2,1)S(1)} %collective-permute-done.2.from1, ...), custom_call_target="tpu_custom_call" | custom-call | tf_op jit(solution)/shard_map/plane/pallas_call | solution.py:447
  20.9 4.6 %collective-permute-start.10 = (bf16[144,128]{1,0:T(8,128)(2,1)S(1)}, bf16[144,128]{1,0:T(8,128)(2,1)S(1)}, u32[]{:S(2)}, u32[]{:S(2)}) collective-permute-start(bf16[144,128]{1,0:T(8,128)(2,1)S(1)} %get-tuple-element.27), channel_id=1, source_target_pairs={{0,128},{4,132},{8,136},{12,140},{16,144},{20,148},{24,152},{28,15... | collective-permute-start | bytes 110600 | tf_op jit(solution)/shard_map/ppermute | solution.py:405
  25.6 3.7 %collective-permute-start.8 = (bf16[144,128]{1,0:T(8,128)(2,1)S(1)}, bf16[144,128]{1,0:T(8,128)(2,1)S(1)}, u32[]{:S(2)}, u32[]{:S(2)}) collective-permute-start(bf16[144,128]{1,0:T(8,128)(2,1)S(1)} %get-tuple-element.27), channel_id=1, source_target_pairs={{0,64},{4,68},{8,72},{12,76},{16,80},{20,84},{24,88},{28,92},{32,9... | collective-permute-start | bytes 110600 | tf_op jit(solution)/shard_map/ppermute | solution.py:405
  29.2 2.3 %collective-permute-start.7 = (bf16[144,128]{1,0:T(8,128)(2,1)S(1)}, bf16[144,128]{1,0:T(8,128)(2,1)S(1)}, u32[]{:S(2)}, u32[]{:S(2)}) collective-permute-start(bf16[144,128]{1,0:T(8,128)(2,1)S(1)} %get-tuple-element.27), channel_id=1, source_target_pairs={{0,32},{4,36},{8,40},{12,44},{16,48},{20,52},{24,56},{28,60},{32,6... | collective-permute-start | bytes 110600 | tf_op jit(solution)/shard_map/ppermute | solution.py:405
  31.5 1.9 %inside.1 = (f32[384,512]{1,0:T(8,128)S(1)}, bf16[384,512]{1,0:T(8,128)(2,1)S(1)}) custom-call(s32[8]{0:T(128)S(1)} %get-tuple-element.23.info, bf16[2,192,512]{2,1,0:T(8,128)(2,1)S(1)} %get-tuple-element.41.keep, bf16[2,192,512]{2,1,0:T(8,128)(2,1)S(1)} %collective-permute-done.6.queries_r, bf16[384,256]{1,0:T(8,128)(2,1)S(1)} %get-tuple-element.28.packed), custom_call_target="tpu_custom_call" | custom-call | tf_op jit(solution)/shard_map/inside/pallas_call | solution.py:462
  33.5 1.2 collective-permute-done.7.from1
  34.7 1.6 %first.1 = (f32[384,512]{1,0:T(8,128)S(1)}, f32[8,8,384]{2,1,0:T(8,128)S(1)}, s32[1]{0:T(128)}) custom-call(s32[8]{0:T(128)S(1)} %get-tuple-element.23.info, f32[136,128]{1,0:T(8,128)S(1)} %get-tuple-element.26.prefix, bf16[144,128]{1,0:T(8,128)(2,1)S(1)} %collective-permute-done.7.from1, bf16[144,128]{1,0:T(8,128)(2,1)S(1)} %collective-permute-done.8.from2, ...), custom_call_target="tpu_custom_call" | custom-call | tf_op jit(solution)/shard_map/first/pallas_call | solution.py:469
  36.9 3.6 %collective-permute-start.12 = (bf16[384,256]{1,0:T(8,128)(2,1)S(1)}, bf16[384,256]{1,0:T(8,128)(2,1)}, u32[]{:S(2)}, u32[]{:S(2)}) collective-permute-start(bf16[384,256]{1,0:T(8,128)(2,1)S(1)} %broadcast_select_fusion.3), channel_id=1, source_target_pairs={{0,128},{4,132},{8,136},{12,140},{16,144},{20,148},{24,152},{28,15... | collective-permute-start | bytes 589832 | tf_op jit(solution)/shard_map/ppermute | solution.py:405
  40.5 21.7 %collective-permute-done.12.own4 = bf16[384,256]{1,0:T(8,128)(2,1)} collective-permute-done((bf16[384,256]{1,0:T(8,128)(2,1)S(1)}, bf16[384,256]{1,0:T(8,128)(2,1)}, u32[]{:S(2)}, u32[]{:S(2)}) %collective-permute-start.12) | collective-permute-done | bytes 196640 | tf_op jit(solution)/shard_map/ppermute | solution.py:405
  62.1 2.4 %collective-permute-start.15 = (bf16[384,256]{1,0:T(8,128)(2,1)}, bf16[384,256]{1,0:T(8,128)(2,1)S(1)}, u32[]{:S(2)}, u32[]{:S(2)}) collective-permute-start(bf16[384,256]{1,0:T(8,128)(2,1)} %collective-permute-done.12.own4), channel_id=1, source_target_pairs={{8,0},{12,4},{16,8},{20,12},{24,16},{28,20},{40,32},{44,36},{48,40... | collective-permute-start | bytes 589832 | tf_op jit(solution)/shard_map/ppermute | solution.py:405
  66.1 2.1 %collective-permute-start.16 = (bf16[768,256]{1,0:T(8,128)(2,1)}, bf16[768,256]{1,0:T(8,128)(2,1)S(1)}, u32[]{:S(2)}, u32[]{:S(2)}) collective-permute-start(bf16[768,256]{1,0:T(8,128)(2,1)} %broadcast_select_fusion), channel_id=1, source_target_pairs={{0,8},{4,12},{8,16},{12,20},{16,24},{20,28},{24,0},{28,4},{32,40},... | collective-permute-start | bytes 1179656 | tf_op jit(solution)/shard_map/ppermute | solution.py:405
  68.1 4.8 %collective-permute-start.14 = (bf16[384,256]{1,0:T(8,128)(2,1)}, bf16[384,256]{1,0:T(8,128)(2,1)}, u32[]{:S(2)}, u32[]{:S(2)}) collective-permute-start(bf16[384,256]{1,0:T(8,128)(2,1)} %collective-permute-done.12.own4), channel_id=1, source_target_pairs={{16,0},{20,4},{24,8},{28,12},{48,32},{52,36},{56,40},{60,44},{80,6... | collective-permute-start | bytes 589832 | tf_op jit(solution)/shard_map/ppermute | solution.py:405
  73.6 2.0 %collective-permute-start.13 = (bf16[384,256]{1,0:T(8,128)(2,1)}, bf16[384,256]{1,0:T(8,128)(2,1)}, u32[]{:S(2)}, u32[]{:S(2)}) collective-permute-start(bf16[384,256]{1,0:T(8,128)(2,1)} %collective-permute-done.12.own4), channel_id=1, source_target_pairs={{24,0},{28,4},{56,32},{60,36},{88,64},{92,68},{120,96},{124,100},{... | collective-permute-start | bytes 589832 | tf_op jit(solution)/shard_map/ppermute | solution.py:405
  75.6 12.1 %all_to_all.10.sums = f32[8,8,384]{2,1,0:T(8,128)S(1)} all-to-all(f32[8,8,384]{2,1,0:T(8,128)S(1)} %get-tuple-element.32), channel_id=1, replica_groups=mesh['z'=8,'x'=4,'core'=2,'tp'=4] {'core','tp'}, dimensions={0} | all-to-all | bytes 196608 | tf_op jit(solution)/shard_map/all_to_all | solution.py:413
  87.7 1.4 %copy-done = bf16[3072,256]{1,0:T(8,128)(2,1)S(1)} copy-done((bf16[3072,256]{1,0:T(8,128)(2,1)S(1)}, bf16[3072,256]{1,0:T(8,128)(2,1)}, u32[]{:S(2)}) %copy-start) | copy-done | bytes 1572888
  89.1 11.5 %near.1 = (bf16[4,384,128]{2,1,0:T(8,128)(2,1)S(1)}, f32[4,384,128]{2,1,0:T(8,128)S(1)}, f32[4,384,256]{2,1,0:T(8,128)S(1)}) custom-call(s32[8]{0:T(128)S(1)} %get-tuple-element.23.info, s32[1]{0:T(128)} %get-tuple-element.31.reach, f32[8,8,384]{2,1,0:T(8,128)S(1)} %all_to_all.10.sums, f32[384,512]{1,0:T(8,128)S(1)} %get-tuple-element.33.first, ...), custom_call_target="tpu_custom_call" | custom-call | tf_op jit(solution)/shard_map/near/pallas_call | solution.py:489
  100.6 7.0 %far.1 = (bf16[192,512]{1,0:T(8,128)(2,1)S(1)}, bf16[192,512]{1,0:T(8,128)(2,1)S(1)}, f32[8,8,192]{2,1,0:T(8,128)S(1)}, f32[4,384,128]{2,1,0:T(8,128)S(1)}, f32[4,384,256]{2,1,0:T(8,128)S(1)}) custom-call(s32[8]{0:T(128)S(1)} %get-tuple-element.23.info, s32[1]{0:T(128)} %get-tuple-element.31.reach, ...), custom_call_target="tpu_custom_call", output_to_operand_aliasing={{3}: (3, {}), {4}: (4, {})} | custom-call | tf_op jit(solution)/shard_map/far/pallas_call | solution.py:507
  108.0 7.7 %all_to_all.11.sums = f32[8,8,192]{2,1,0:T(8,128)S(1)} all-to-all(f32[8,8,192]{2,1,0:T(8,128)S(1)} %get-tuple-element.38), channel_id=1, replica_groups=mesh['z'=8,'x'=4,'core'=2,'tp'=4] {'core','tp'}, dimensions={0} | all-to-all | bytes 98304 | tf_op jit(solution)/shard_map/all_to_all | solution.py:413
  115.7 1.0 last.1
  (47 shorter events, 8.6 us)
Async XLA Ops:
  6.5 2.7 %copy-start.4 = (bf16[192,1024]{1,0:T(8,128)(2,1)S(1)}, bf16[192,1024]{1,0:T(8,128)(2,1)}, u32[]{:S(2)}) copy-start(bf16[192,1024]{1,0:T(8,128)(2,1)} %param.11) | copy-start | bytes 1179652
  6.5 2.7 %copy-start.5 = (bf16[192,1024]{1,0:T(8,128)(2,1)S(1)}, bf16[192,1024]{1,0:T(8,128)(2,1)}, u32[]{:S(2)}) copy-start(bf16[192,1024]{1,0:T(8,128)(2,1)} %param.7) | copy-start | bytes 1179652
  6.5 81.1 %all-gather.2.cloned.1.call-start = ((), (), s32[]{:S(2)}) async-start(), calls=%async_computation.2 | async-start | bytes 1966080 | tf_op jit(solution)/shard_map/all_gather | solution.py:460
  8.5 2.7 %collective-permute-start.1 = (bf16[4,192,128]{2,1,0:T(8,128)(2,1)S(1)}, bf16[4,192,128]{2,1,0:T(8,128)(2,1)S(1)}, u32[]{:S(2)}, u32[]{:S(2)}) collective-permute-start(bf16[4,192,128]{2,1,0:T(8,128)(2,1)S(1)} %get-tuple-element.47), channel_id=1, source_target_pairs={{0,4},{4,0},{8,12},{12,8},{16,20},{20,16},{24,28},{28,24},{32,36},... | collective-permute-start | bytes 589832 | tf_op jit(solution)/shard_map/ppermute | solution.py:405
  9.4 10.2 %collective-permute-start.6 = (bf16[2,192,512]{2,1,0:T(8,128)(2,1)S(1)}, bf16[2,192,512]{2,1,0:T(8,128)(2,1)S(1)}, u32[]{:S(2)}, u32[]{:S(2)}) collective-permute-start(bf16[2,192,512]{2,1,0:T(8,128)(2,1)S(1)} %get-tuple-element.42), channel_id=1, source_target_pairs={{0,4},{4,0},{8,12},{12,8},{16,20},{20,16},{24,28},{28,24},{32,36},... | collective-permute-start | bytes 1179656 | tf_op jit(solution)/shard_map/ppermute | solution.py:405
  9.5 1.7 %collective-permute-start = (s32[192]{0:T(256)S(1)}, s32[192]{0:T(256)S(1)}, u32[]{:S(2)}, u32[]{:S(2)}) collective-permute-start(s32[192]{0:T(256)S(1)} %copy-done.3), channel_id=1, source_target_pairs={{0,4},{4,0},{8,12},{12,8},{16,20},{20,16},{24,28},{28,24},{32,36},... | collective-permute-start | bytes 2312 | tf_op jit(solution)/shard_map/ppermute | solution.py:405
  12.6 7.0 %collective-permute-start.5 = (bf16[384,256]{1,0:T(8,128)(2,1)S(1)}, bf16[384,256]{1,0:T(8,128)(2,1)S(1)}, u32[]{:S(2)}, u32[]{:S(2)}) collective-permute-start(bf16[384,256]{1,0:T(8,128)(2,1)S(1)} %get-tuple-element.25.own0), channel_id=1, source_target_pairs={{0,32},{4,36},{8,40},{12,44},{16,48},{20,52},{24,56},{28,60},{32,6... | collective-permute-start | bytes 589832 | tf_op jit(solution)/shard_map/ppermute | solution.py:405
  14.3 4.0 %collective-permute-start.4 = (bf16[144,128]{1,0:T(8,128)(2,1)S(1)}, bf16[144,128]{1,0:T(8,128)(2,1)S(1)}, u32[]{:S(2)}, u32[]{:S(2)}) collective-permute-start(bf16[144,128]{1,0:T(8,128)(2,1)S(1)} %get-tuple-element.24.own), channel_id=1, source_target_pairs={{0,24},{4,28},{8,0},{12,4},{16,8},{20,12},{24,16},{28,20},{32,56},... | collective-permute-start | bytes 110600 | tf_op jit(solution)/shard_map/ppermute | solution.py:405
  14.8 4.3 %collective-permute-start.3 = (bf16[144,128]{1,0:T(8,128)(2,1)S(1)}, bf16[144,128]{1,0:T(8,128)(2,1)S(1)}, u32[]{:S(2)}, u32[]{:S(2)}) collective-permute-start(bf16[144,128]{1,0:T(8,128)(2,1)S(1)} %get-tuple-element.24.own), channel_id=1, source_target_pairs={{0,16},{4,20},{8,24},{12,28},{16,0},{20,4},{24,8},{28,12},{32,48},... | collective-permute-start | bytes 110600 | tf_op jit(solution)/shard_map/ppermute | solution.py:405
  15.7 3.9 %collective-permute-start.2 = (bf16[144,128]{1,0:T(8,128)(2,1)S(1)}, bf16[144,128]{1,0:T(8,128)(2,1)S(1)}, u32[]{:S(2)}, u32[]{:S(2)}) collective-permute-start(bf16[144,128]{1,0:T(8,128)(2,1)S(1)} %get-tuple-element.24.own), channel_id=1, source_target_pairs={{0,8},{4,12},{8,16},{12,20},{16,24},{20,28},{24,0},{28,4},{32,40},... | collective-permute-start | bytes 110600 | tf_op jit(solution)/shard_map/ppermute | solution.py:405
  20.9 12.5 %collective-permute-start.10 = (bf16[144,128]{1,0:T(8,128)(2,1)S(1)}, bf16[144,128]{1,0:T(8,128)(2,1)S(1)}, u32[]{:S(2)}, u32[]{:S(2)}) collective-permute-start(bf16[144,128]{1,0:T(8,128)(2,1)S(1)} %get-tuple-element.27), channel_id=1, source_target_pairs={{0,128},{4,132},{8,136},{12,140},{16,144},{20,148},{24,152},{28,15... | collective-permute-start | bytes 110600 | tf_op jit(solution)/shard_map/ppermute | solution.py:405
  25.6 7.9 %collective-permute-start.9 = (bf16[144,128]{1,0:T(8,128)(2,1)S(1)}, bf16[144,128]{1,0:T(8,128)(2,1)S(1)}, u32[]{:S(2)}, u32[]{:S(2)}) collective-permute-start(bf16[144,128]{1,0:T(8,128)(2,1)S(1)} %get-tuple-element.27), channel_id=1, source_target_pairs={{0,96},{4,100},{8,104},{12,108},{16,112},{20,116},{24,120},{28,124... | collective-permute-start | bytes 110600 | tf_op jit(solution)/shard_map/ppermute | solution.py:405
  25.6 7.9 %collective-permute-start.8 = (bf16[144,128]{1,0:T(8,128)(2,1)S(1)}, bf16[144,128]{1,0:T(8,128)(2,1)S(1)}, u32[]{:S(2)}, u32[]{:S(2)}) collective-permute-start(bf16[144,128]{1,0:T(8,128)(2,1)S(1)} %get-tuple-element.27), channel_id=1, source_target_pairs={{0,64},{4,68},{8,72},{12,76},{16,80},{20,84},{24,88},{28,92},{32,9... | collective-permute-start | bytes 110600 | tf_op jit(solution)/shard_map/ppermute | solution.py:405
  29.2 5.4 %collective-permute-start.7 = (bf16[144,128]{1,0:T(8,128)(2,1)S(1)}, bf16[144,128]{1,0:T(8,128)(2,1)S(1)}, u32[]{:S(2)}, u32[]{:S(2)}) collective-permute-start(bf16[144,128]{1,0:T(8,128)(2,1)S(1)} %get-tuple-element.27), channel_id=1, source_target_pairs={{0,32},{4,36},{8,40},{12,44},{16,48},{20,52},{24,56},{28,60},{32,6... | collective-permute-start | bytes 110600 | tf_op jit(solution)/shard_map/ppermute | solution.py:405
  31.5 33.0 %collective-permute-start.11 = (bf16[768,256]{1,0:T(8,128)(2,1)}, bf16[768,256]{1,0:T(8,128)(2,1)S(1)}, u32[]{:S(2)}, u32[]{:S(2)}) collective-permute-start(bf16[768,256]{1,0:T(8,128)(2,1)} %get-tuple-element.34), channel_id=1, source_target_pairs={{0,64},{4,68},{8,72},{12,76},{16,80},{20,84},{24,88},{28,92},{32,9... | collective-permute-start | bytes 1179656 | tf_op jit(solution)/shard_map/ppermute | solution.py:405
  36.9 25.3 %collective-permute-start.12 = (bf16[384,256]{1,0:T(8,128)(2,1)S(1)}, bf16[384,256]{1,0:T(8,128)(2,1)}, u32[]{:S(2)}, u32[]{:S(2)}) collective-permute-start(bf16[384,256]{1,0:T(8,128)(2,1)S(1)} %broadcast_select_fusion.3), channel_id=1, source_target_pairs={{0,128},{4,132},{8,136},{12,140},{16,144},{20,148},{24,152},{28,15... | collective-permute-start | bytes 589832 | tf_op jit(solution)/shard_map/ppermute | solution.py:405
  62.1 10.8 %collective-permute-start.15 = (bf16[384,256]{1,0:T(8,128)(2,1)}, bf16[384,256]{1,0:T(8,128)(2,1)S(1)}, u32[]{:S(2)}, u32[]{:S(2)}) collective-permute-start(bf16[384,256]{1,0:T(8,128)(2,1)} %collective-permute-done.12.own4), channel_id=1, source_target_pairs={{8,0},{12,4},{16,8},{20,12},{24,16},{28,20},{40,32},{44,36},{48,40... | collective-permute-start | bytes 589832 | tf_op jit(solution)/shard_map/ppermute | solution.py:405
  65.3 35.3 %collective-permute-start.18 = (bf16[768,256]{1,0:T(8,128)(2,1)}, bf16[768,256]{1,0:T(8,128)(2,1)S(1)}, u32[]{:S(2)}, u32[]{:S(2)}) collective-permute-start(bf16[768,256]{1,0:T(8,128)(2,1)} %broadcast_select_fusion), channel_id=1, source_target_pairs={{0,24},{4,28},{8,0},{12,4},{16,8},{20,12},{24,16},{28,20},{32,56},... | collective-permute-start | bytes 1179656 | tf_op jit(solution)/shard_map/ppermute | solution.py:405
  65.7 34.9 %collective-permute-start.17 = (bf16[768,256]{1,0:T(8,128)(2,1)}, bf16[768,256]{1,0:T(8,128)(2,1)S(1)}, u32[]{:S(2)}, u32[]{:S(2)}) collective-permute-start(bf16[768,256]{1,0:T(8,128)(2,1)} %broadcast_select_fusion), channel_id=1, source_target_pairs={{0,16},{4,20},{8,24},{12,28},{16,0},{20,4},{24,8},{28,12},{32,48},... | collective-permute-start | bytes 1179656 | tf_op jit(solution)/shard_map/ppermute | solution.py:405
  66.1 34.5 %collective-permute-start.16 = (bf16[768,256]{1,0:T(8,128)(2,1)}, bf16[768,256]{1,0:T(8,128)(2,1)S(1)}, u32[]{:S(2)}, u32[]{:S(2)}) collective-permute-start(bf16[768,256]{1,0:T(8,128)(2,1)} %broadcast_select_fusion), channel_id=1, source_target_pairs={{0,8},{4,12},{8,16},{12,20},{16,24},{20,28},{24,0},{28,4},{32,40},... | collective-permute-start | bytes 1179656 | tf_op jit(solution)/shard_map/ppermute | solution.py:405
  68.1 32.4 %collective-permute-start.14 = (bf16[384,256]{1,0:T(8,128)(2,1)}, bf16[384,256]{1,0:T(8,128)(2,1)}, u32[]{:S(2)}, u32[]{:S(2)}) collective-permute-start(bf16[384,256]{1,0:T(8,128)(2,1)} %collective-permute-done.12.own4), channel_id=1, source_target_pairs={{16,0},{20,4},{24,8},{28,12},{48,32},{52,36},{56,40},{60,44},{80,6... | collective-permute-start | bytes 589832 | tf_op jit(solution)/shard_map/ppermute | solution.py:405
  73.6 27.0 %collective-permute-start.13 = (bf16[384,256]{1,0:T(8,128)(2,1)}, bf16[384,256]{1,0:T(8,128)(2,1)}, u32[]{:S(2)}, u32[]{:S(2)}) collective-permute-start(bf16[384,256]{1,0:T(8,128)(2,1)} %collective-permute-done.12.own4), channel_id=1, source_target_pairs={{24,0},{28,4},{56,32},{60,36},{88,64},{92,68},{120,96},{124,100},{... | collective-permute-start | bytes 589832 | tf_op jit(solution)/shard_map/ppermute | solution.py:405
  89.1 11.5 %copy-start.2 = (bf16[384,256]{1,0:T(8,128)(2,1)S(1)}, bf16[384,256]{1,0:T(8,128)(2,1)}, u32[]{:S(2)}) copy-start(bf16[384,256]{1,0:T(8,128)(2,1)} %copy-done.1) | copy-start | bytes 589828
  107.6 8.1 %collective-permute-start.19 = (bf16[192,512]{1,0:T(8,128)(2,1)S(1)}, bf16[192,512]{1,0:T(8,128)(2,1)S(1)}, u32[]{:S(2)}, u32[]{:S(2)}) collective-permute-start(bf16[192,512]{1,0:T(8,128)(2,1)S(1)} %get-tuple-element.40), channel_id=1, source_target_pairs={{0,4},{4,0},{8,12},{12,8},{16,20},{20,16},{24,28},{28,24},{32,36},... | collective-permute-start | bytes 589832 | tf_op jit(solution)/shard_map/ppermute | solution.py:405
  (3 other events, 3.1 us)
Sparse Core Ops, SparseCore 0:
  21.0 30.7 all-gather.1
